TPU v7x, 512 devices: a whole 4x8x8 slice. The times are simulated.
512 devices in a mesh: loop: 32 (over y_hi, x, core), grp: 16 (over y_lo, z).
Axes of the slice: x: 4, y: 8 (y_hi: 4, y_lo: 2; y = y_hi * 2 + y_lo), z: 8, core: 2. Of those that a mesh axis runs over, the one named last changes fastest.
Arguments:
- image_emb: bfloat16 [8192, 1152], P(('loop', 'grp')), may hold values from -6 to 6
- text_emb: bfloat16 [8192, 1152], P(('loop', 'grp')), may hold values from -6 to 6
- log_scale: float32 [1], replicated, may hold values from 4.2 to 4.8
- bias: float32 [1], replicated, may hold values from -4 to -2
Outputs:
- image_grad: float32 [8192, 1152], P(('loop', 'grp'))
- text_grad: float32 [8192, 1152], P(('loop', 'grp'))
All inputs are finite; a program needn't handle non-finite values.
Results may differ from a plain program's by a relative error of at most 0.008.
Values may be sent and summed in bfloat16 or wider, within the bound.
A program may use at most 64 MiB of HBM per device.

v0:
```python
import jax
import jax.numpy as jnp
from jax import lax
from jax.sharding import PartitionSpec as P

EPS = 1e-06


def from_behind(value, axis, steps):
    count = lax.axis_size(axis)
    pairs = [(source, (source + steps) % count) for source in range(count)]
    return lax.ppermute(value, axis, pairs)


def normalize(values):
    wide = values.astype(jnp.float32)
    length = jnp.sqrt(jnp.sum(wide * wide, axis=-1, keepdims=True) + EPS)
    return (wide / length, length)


def norm_back(unit_rows, length, upstream):
    along = jnp.sum(unit_rows * upstream, axis=-1, keepdims=True)
    return (upstream - unit_rows * along) / length


def move_text(text_rows):
    return from_behind(text_rows, "loop", 1)


def move_grads(text_grad):
    return from_behind(text_grad, "loop", 1)


def per_device(image_emb, text_emb, log_scale, bias):
    row_count, feat_width = image_emb.shape
    loop_count = lax.axis_size("loop")
    groups = lax.axis_size("grp")
    loop_at = lax.axis_index("loop")
    group_at = lax.axis_index("grp")
    logit_scale = jnp.exp(log_scale[0])
    offset = bias[0]
    img_unit, img_length = normalize(image_emb)
    txt_unit, txt_length = normalize(text_emb)
    image_block = lax.all_gather(img_unit.astype(jnp.bfloat16), "grp", axis=0, tiled=True)
    block_rows = groups * row_count
    image_ids = loop_at * block_rows + jnp.arange(block_rows, dtype=jnp.int32)
    text_rows = txt_unit.astype(jnp.bfloat16)

    def text_ids(turn_index):
        source = (loop_at - turn_index) % loop_count
        return (source * groups + group_at) * row_count + jnp.arange(row_count, dtype=jnp.int32)

    def station(turn_index, moving, summed, grads_seen, texts_seen):
        logits = (
            logit_scale
            * jnp.einsum("id,kd->ik", image_block, moving, preferred_element_type=jnp.float32)
            + offset
        )
        labels = (image_ids[:, None] == text_ids(turn_index)[None, :]).astype(jnp.float32)
        grad_low = (logit_scale * (jax.nn.sigmoid(logits) - labels)).astype(jnp.bfloat16)
        summed = summed + jnp.einsum(
            "ik,id->kd", grad_low, image_block, preferred_element_type=jnp.float32
        )
        grads_seen = lax.dynamic_update_slice(grads_seen, grad_low, (0, turn_index * row_count))
        texts_seen = lax.dynamic_update_slice(texts_seen, moving, (turn_index * row_count, 0))
        return (summed, grads_seen, texts_seen)

    text_grad = jnp.zeros((row_count, feat_width), jnp.float32)
    grad_table = jnp.zeros((block_rows, loop_count * row_count), jnp.bfloat16)
    text_table = jnp.zeros((loop_count * row_count, feat_width), jnp.bfloat16)
    text_grad, grad_table, text_table = station(
        jnp.int32(0), text_rows, text_grad, grad_table, text_table
    )

    def turn(turn_index, loop_state):
        moving, summed, grads_seen, texts_seen = loop_state
        moving = move_text(moving)
        summed = move_grads(summed)
        summed, grads_seen, texts_seen = station(turn_index, moving, summed, grads_seen, texts_seen)
        return (moving, summed, grads_seen, texts_seen)

    text_rows, text_grad, grad_table, text_table = lax.fori_loop(
        1, loop_count, turn, (text_rows, text_grad, grad_table, text_table)
    )
    text_grad = move_grads(text_grad)
    image_terms = jnp.dot(grad_table, text_table, preferred_element_type=jnp.float32)
    image_sum = lax.psum_scatter(image_terms, "grp", scatter_dimension=0, tiled=True)
    return (norm_back(img_unit, img_length, image_sum), norm_back(txt_unit, txt_length, text_grad))


def solution(mesh):
    return jax.shard_map(
        per_device,
        mesh=mesh,
        in_specs=(P(("loop", "grp"), None), P(("loop", "grp"), None), P(), P()),
        out_specs=(P(("loop", "grp"), None), P(("loop", "grp"), None)),
        check_vma=False,
    )
```

profile of v0, /device:TPU:4, one launch (start us, length us, event | category | flops | bytes accessed | tf_op | source)
XLA Modules:
  0.0 511.3 jit_solution(7196596203872255199)
XLA Ops:
  12.1 42.7 %all_gather.3 = bf16[256,1152]{1,0:T(8,128)(2,1)S(1)} all-gather(bf16[16,1152]{1,0:T(8,128)(2,1)S(1)} %fusion.21), channel_id=1, replica_groups=mesh['loop'=32,'grp'=16] {'grp'}, dimensions={0}, use_global_device_ids=true | all-gather | bytes 626688 | tf_op jit(solution)/shard_map/all_gather | solution.py:44
  55.4 350.3 %while.22 = (s32[]{:T(128)}, bf16[16,1152]{1,0:T(8,128)(2,1)S(1)}, f32[16,1152]{1,0:T(8,128)S(1)}, bf16[256,512]{0,1:T(8,128)(2,1)S(1)}, bf16[512,1152]{1,0:T(8,...) while((s32[]{:T(128)}, bf16[16,1152]{1,0:T(8,128)(2,1)S(1)}, ...), condition=%wide.region_3.4_spmd.clone, body=%wide.region_2.3_spmd.clone.sunk | while | flops 18934052 | bytes 1981456 | solution.py:82
  57.3 3.2 collective-permute-start.1
  65.2 3.2 collective-permute-start.1
  73.0 6.9 %collective-permute-start.1 = (f32[16,1152]{1,0:T(8,128)S(1)}, f32[16,1152]{1,0:T(8,128)S(1)}, u32[]{:S(2)}, u32[]{:S(2)}) collective-permute-start(f32[16,1152]{1,0:T(8,128)S(1)} %get-tuple-element.411), channel_id=1, source_target_pairs={{0,16},{16,32},{32,48},{48,64},{64,80},{80,96},{96,112},{112,128},... | collective-permute-start | bytes 221192 | tf_op jit(solution)/shard_map/while/body/eval_jaxpr/ppermute | solution.py:12
  83.7 7.8 %collective-permute-start.1 = (f32[16,1152]{1,0:T(8,128)S(1)}, f32[16,1152]{1,0:T(8,128)S(1)}, u32[]{:S(2)}, u32[]{:S(2)}) collective-permute-start(f32[16,1152]{1,0:T(8,128)S(1)} %get-tuple-element.411), channel_id=1, source_target_pairs={{0,16},{16,32},{32,48},{48,64},{64,80},{80,96},{96,112},{112,128},... | collective-permute-start | bytes 221192 | tf_op jit(solution)/shard_map/while/body/eval_jaxpr/ppermute | solution.py:12
  95.3 7.0 %collective-permute-start.1 = (f32[16,1152]{1,0:T(8,128)S(1)}, f32[16,1152]{1,0:T(8,128)S(1)}, u32[]{:S(2)}, u32[]{:S(2)}) collective-permute-start(f32[16,1152]{1,0:T(8,128)S(1)} %get-tuple-element.411), channel_id=1, source_target_pairs={{0,16},{16,32},{32,48},{48,64},{64,80},{80,96},{96,112},{112,128},... | collective-permute-start | bytes 221192 | tf_op jit(solution)/shard_map/while/body/eval_jaxpr/ppermute | solution.py:12
  106.4 7.1 %collective-permute-start.1 = (f32[16,1152]{1,0:T(8,128)S(1)}, f32[16,1152]{1,0:T(8,128)S(1)}, u32[]{:S(2)}, u32[]{:S(2)}) collective-permute-start(f32[16,1152]{1,0:T(8,128)S(1)} %get-tuple-element.411), channel_id=1, source_target_pairs={{0,16},{16,32},{32,48},{48,64},{64,80},{80,96},{96,112},{112,128},... | collective-permute-start | bytes 221192 | tf_op jit(solution)/shard_map/while/body/eval_jaxpr/ppermute | solution.py:12
  117.4 7.0 %collective-permute-start.1 = (f32[16,1152]{1,0:T(8,128)S(1)}, f32[16,1152]{1,0:T(8,128)S(1)}, u32[]{:S(2)}, u32[]{:S(2)}) collective-permute-start(f32[16,1152]{1,0:T(8,128)S(1)} %get-tuple-element.411), channel_id=1, source_target_pairs={{0,16},{16,32},{32,48},{48,64},{64,80},{80,96},{96,112},{112,128},... | collective-permute-start | bytes 221192 | tf_op jit(solution)/shard_map/while/body/eval_jaxpr/ppermute | solution.py:12
  128.2 7.0 %collective-permute-start.1 = (f32[16,1152]{1,0:T(8,128)S(1)}, f32[16,1152]{1,0:T(8,128)S(1)}, u32[]{:S(2)}, u32[]{:S(2)}) collective-permute-start(f32[16,1152]{1,0:T(8,128)S(1)} %get-tuple-element.411), channel_id=1, source_target_pairs={{0,16},{16,32},{32,48},{48,64},{64,80},{80,96},{96,112},{112,128},... | collective-permute-start | bytes 221192 | tf_op jit(solution)/shard_map/while/body/eval_jaxpr/ppermute | solution.py:12
  139.0 7.0 %collective-permute-start.1 = (f32[16,1152]{1,0:T(8,128)S(1)}, f32[16,1152]{1,0:T(8,128)S(1)}, u32[]{:S(2)}, u32[]{:S(2)}) collective-permute-start(f32[16,1152]{1,0:T(8,128)S(1)} %get-tuple-element.411), channel_id=1, source_target_pairs={{0,16},{16,32},{32,48},{48,64},{64,80},{80,96},{96,112},{112,128},... | collective-permute-start | bytes 221192 | tf_op jit(solution)/shard_map/while/body/eval_jaxpr/ppermute | solution.py:12
  149.8 7.0 %collective-permute-start.1 = (f32[16,1152]{1,0:T(8,128)S(1)}, f32[16,1152]{1,0:T(8,128)S(1)}, u32[]{:S(2)}, u32[]{:S(2)}) collective-permute-start(f32[16,1152]{1,0:T(8,128)S(1)} %get-tuple-element.411), channel_id=1, source_target_pairs={{0,16},{16,32},{32,48},{48,64},{64,80},{80,96},{96,112},{112,128},... | collective-permute-start | bytes 221192 | tf_op jit(solution)/shard_map/while/body/eval_jaxpr/ppermute | solution.py:12
  160.6 7.0 %collective-permute-start.1 = (f32[16,1152]{1,0:T(8,128)S(1)}, f32[16,1152]{1,0:T(8,128)S(1)}, u32[]{:S(2)}, u32[]{:S(2)}) collective-permute-start(f32[16,1152]{1,0:T(8,128)S(1)} %get-tuple-element.411), channel_id=1, source_target_pairs={{0,16},{16,32},{32,48},{48,64},{64,80},{80,96},{96,112},{112,128},... | collective-permute-start | bytes 221192 | tf_op jit(solution)/shard_map/while/body/eval_jaxpr/ppermute | solution.py:12
  171.5 7.0 %collective-permute-start.1 = (f32[16,1152]{1,0:T(8,128)S(1)}, f32[16,1152]{1,0:T(8,128)S(1)}, u32[]{:S(2)}, u32[]{:S(2)}) collective-permute-start(f32[16,1152]{1,0:T(8,128)S(1)} %get-tuple-element.411), channel_id=1, source_target_pairs={{0,16},{16,32},{32,48},{48,64},{64,80},{80,96},{96,112},{112,128},... | collective-permute-start | bytes 221192 | tf_op jit(solution)/shard_map/while/body/eval_jaxpr/ppermute | solution.py:12
  182.3 7.0 %collective-permute-start.1 = (f32[16,1152]{1,0:T(8,128)S(1)}, f32[16,1152]{1,0:T(8,128)S(1)}, u32[]{:S(2)}, u32[]{:S(2)}) collective-permute-start(f32[16,1152]{1,0:T(8,128)S(1)} %get-tuple-element.411), channel_id=1, source_target_pairs={{0,16},{16,32},{32,48},{48,64},{64,80},{80,96},{96,112},{112,128},... | collective-permute-start | bytes 221192 | tf_op jit(solution)/shard_map/while/body/eval_jaxpr/ppermute | solution.py:12
  190.5 3.1 collective-permute-start
  193.7 7.1 %collective-permute-start.1 = (f32[16,1152]{1,0:T(8,128)S(1)}, f32[16,1152]{1,0:T(8,128)S(1)}, u32[]{:S(2)}, u32[]{:S(2)}) collective-permute-start(f32[16,1152]{1,0:T(8,128)S(1)} %get-tuple-element.411), channel_id=1, source_target_pairs={{0,16},{16,32},{32,48},{48,64},{64,80},{80,96},{96,112},{112,128},... | collective-permute-start | bytes 221192 | tf_op jit(solution)/shard_map/while/body/eval_jaxpr/ppermute | solution.py:12
  204.6 7.8 %collective-permute-start.1 = (f32[16,1152]{1,0:T(8,128)S(1)}, f32[16,1152]{1,0:T(8,128)S(1)}, u32[]{:S(2)}, u32[]{:S(2)}) collective-permute-start(f32[16,1152]{1,0:T(8,128)S(1)} %get-tuple-element.411), channel_id=1, source_target_pairs={{0,16},{16,32},{32,48},{48,64},{64,80},{80,96},{96,112},{112,128},... | collective-permute-start | bytes 221192 | tf_op jit(solution)/shard_map/while/body/eval_jaxpr/ppermute | solution.py:12
  216.2 7.0 %collective-permute-start.1 = (f32[16,1152]{1,0:T(8,128)S(1)}, f32[16,1152]{1,0:T(8,128)S(1)}, u32[]{:S(2)}, u32[]{:S(2)}) collective-permute-start(f32[16,1152]{1,0:T(8,128)S(1)} %get-tuple-element.411), channel_id=1, source_target_pairs={{0,16},{16,32},{32,48},{48,64},{64,80},{80,96},{96,112},{112,128},... | collective-permute-start | bytes 221192 | tf_op jit(solution)/shard_map/while/body/eval_jaxpr/ppermute | solution.py:12
  227.0 7.0 %collective-permute-start.1 = (f32[16,1152]{1,0:T(8,128)S(1)}, f32[16,1152]{1,0:T(8,128)S(1)}, u32[]{:S(2)}, u32[]{:S(2)}) collective-permute-start(f32[16,1152]{1,0:T(8,128)S(1)} %get-tuple-element.411), channel_id=1, source_target_pairs={{0,16},{16,32},{32,48},{48,64},{64,80},{80,96},{96,112},{112,128},... | collective-permute-start | bytes 221192 | tf_op jit(solution)/shard_map/while/body/eval_jaxpr/ppermute | solution.py:12
  238.6 6.2 %collective-permute-start.1 = (f32[16,1152]{1,0:T(8,128)S(1)}, f32[16,1152]{1,0:T(8,128)S(1)}, u32[]{:S(2)}, u32[]{:S(2)}) collective-permute-start(f32[16,1152]{1,0:T(8,128)S(1)} %get-tuple-element.411), channel_id=1, source_target_pairs={{0,16},{16,32},{32,48},{48,64},{64,80},{80,96},{96,112},{112,128},... | collective-permute-start | bytes 221192 | tf_op jit(solution)/shard_map/while/body/eval_jaxpr/ppermute | solution.py:12
  250.7 5.1 collective-permute-start.1
  262.7 3.9 collective-permute-start.1
  266.7 3.6 collective-permute-done
  274.7 3.5 collective-permute-start.1
  278.3 4.0 collective-permute-done
  286.8 3.5 collective-permute-start.1
  290.3 4.0 collective-permute-done
  298.8 3.5 collective-permute-start.1
  302.4 4.0 collective-permute-done
  310.8 3.5 collective-permute-start.1
  314.4 4.3 collective-permute-done
  323.1 3.2 collective-permute-start.1
  326.4 4.3 collective-permute-done
  335.2 3.2 collective-permute-start.1
  338.4 4.3 collective-permute-done
  347.2 3.2 collective-permute-start.1
  350.5 4.3 collective-permute-done
  359.2 3.2 collective-permute-start.1
  362.5 4.5 collective-permute-done
  371.5 3.0 collective-permute-start.1
  374.5 4.6 collective-permute-done
  383.6 2.9 collective-permute-start.1
  386.6 4.6 collective-permute-done
  395.6 2.9 collective-permute-start.1
  398.6 4.6 collective-permute-done
  409.2 8.1 %collective-permute-done.2 = f32[16,1152]{1,0:T(8,128)S(1)} collective-permute-done((f32[16,1152]{1,0:T(8,128)S(1)}, f32[16,1152]{1,0:T(8,128)S(1)}, u32[]{:S(2)}, u32[]{:S(2)}) %collective-permute-start.2) | collective-permute-done | bytes 73760 | tf_op jit(solution)/shard_map/ppermute | solution.py:12
  418.3 83.5 %reduce-scatter.2.cloned.1.call-done = f32[16,1152]{1,0:T(8,128)} async-done(((f32[256,1152]{1,0:T(8,128)}), f32[16,1152]{1,0:T(8,128)}) %reduce-scatter.2.cloned.1.call-update) | async-done | bytes 73744 | tf_op jit(solution)/shard_map/reduce_scatter | solution.py:87
  (290 shorter events, 140.5 us)
Async XLA Ops:
  7.2 494.6 %reduce-scatter.2.cloned.1.call-start = ((), (), s32[]{:S(2)}) async-start(), calls=%async_computation.1 | async-start | bytes 1253376 | tf_op jit(solution)/shard_map/reduce_scatter | solution.py:87
  71.0 8.9 %collective-permute-start = (bf16[16,1152]{1,0:T(8,128)(2,1)S(1)}, bf16[16,1152]{1,0:T(8,128)(2,1)S(1)}, u32[]{:S(2)}, u32[]{:S(2)}) collective-permute-start(bf16[16,1152]{1,0:T(8,128)(2,1)S(1)} %get-tuple-element.410), channel_id=1, source_target_pairs={{0,16},{16,32},{32,48},{48,64},{64,80},{80,96},{96,112},{112,128},... | collective-permute-start | bytes 110600 | tf_op jit(solution)/shard_map/while/body/eval_jaxpr/ppermute | solution.py:12
  81.2 10.4 %collective-permute-start = (bf16[16,1152]{1,0:T(8,128)(2,1)S(1)}, bf16[16,1152]{1,0:T(8,128)(2,1)S(1)}, u32[]{:S(2)}, u32[]{:S(2)}) collective-permute-start(bf16[16,1152]{1,0:T(8,128)(2,1)S(1)} %get-tuple-element.410), channel_id=1, source_target_pairs={{0,16},{16,32},{32,48},{48,64},{64,80},{80,96},{96,112},{112,128},... | collective-permute-start | bytes 110600 | tf_op jit(solution)/shard_map/while/body/eval_jaxpr/ppermute | solution.py:12
  83.7 8.8 %collective-permute-start.1 = (f32[16,1152]{1,0:T(8,128)S(1)}, f32[16,1152]{1,0:T(8,128)S(1)}, u32[]{:S(2)}, u32[]{:S(2)}) collective-permute-start(f32[16,1152]{1,0:T(8,128)S(1)} %get-tuple-element.411), channel_id=1, source_target_pairs={{0,16},{16,32},{32,48},{48,64},{64,80},{80,96},{96,112},{112,128},... | collective-permute-start | bytes 221192 | tf_op jit(solution)/shard_map/while/body/eval_jaxpr/ppermute | solution.py:12
  92.8 9.6 %collective-permute-start = (bf16[16,1152]{1,0:T(8,128)(2,1)S(1)}, bf16[16,1152]{1,0:T(8,128)(2,1)S(1)}, u32[]{:S(2)}, u32[]{:S(2)}) collective-permute-start(bf16[16,1152]{1,0:T(8,128)(2,1)S(1)} %get-tuple-element.410), channel_id=1, source_target_pairs={{0,16},{16,32},{32,48},{48,64},{64,80},{80,96},{96,112},{112,128},... | collective-permute-start | bytes 110600 | tf_op jit(solution)/shard_map/while/body/eval_jaxpr/ppermute | solution.py:12
  103.6 10.0 %collective-permute-start = (bf16[16,1152]{1,0:T(8,128)(2,1)S(1)}, bf16[16,1152]{1,0:T(8,128)(2,1)S(1)}, u32[]{:S(2)}, u32[]{:S(2)}) collective-permute-start(bf16[16,1152]{1,0:T(8,128)(2,1)S(1)} %get-tuple-element.410), channel_id=1, source_target_pairs={{0,16},{16,32},{32,48},{48,64},{64,80},{80,96},{96,112},{112,128},... | collective-permute-start | bytes 110600 | tf_op jit(solution)/shard_map/while/body/eval_jaxpr/ppermute | solution.py:12
  114.8 9.6 %collective-permute-start = (bf16[16,1152]{1,0:T(8,128)(2,1)S(1)}, bf16[16,1152]{1,0:T(8,128)(2,1)S(1)}, u32[]{:S(2)}, u32[]{:S(2)}) collective-permute-start(bf16[16,1152]{1,0:T(8,128)(2,1)S(1)} %get-tuple-element.410), channel_id=1, source_target_pairs={{0,16},{16,32},{32,48},{48,64},{64,80},{80,96},{96,112},{112,128},... | collective-permute-start | bytes 110600 | tf_op jit(solution)/shard_map/while/body/eval_jaxpr/ppermute | solution.py:12
  125.6 9.6 %collective-permute-start = (bf16[16,1152]{1,0:T(8,128)(2,1)S(1)}, bf16[16,1152]{1,0:T(8,128)(2,1)S(1)}, u32[]{:S(2)}, u32[]{:S(2)}) collective-permute-start(bf16[16,1152]{1,0:T(8,128)(2,1)S(1)} %get-tuple-element.410), channel_id=1, source_target_pairs={{0,16},{16,32},{32,48},{48,64},{64,80},{80,96},{96,112},{112,128},... | collective-permute-start | bytes 110600 | tf_op jit(solution)/shard_map/while/body/eval_jaxpr/ppermute | solution.py:12
  136.4 9.6 %collective-permute-start = (bf16[16,1152]{1,0:T(8,128)(2,1)S(1)}, bf16[16,1152]{1,0:T(8,128)(2,1)S(1)}, u32[]{:S(2)}, u32[]{:S(2)}) collective-permute-start(bf16[16,1152]{1,0:T(8,128)(2,1)S(1)} %get-tuple-element.410), channel_id=1, source_target_pairs={{0,16},{16,32},{32,48},{48,64},{64,80},{80,96},{96,112},{112,128},... | collective-permute-start | bytes 110600 | tf_op jit(solution)/shard_map/while/body/eval_jaxpr/ppermute | solution.py:12
  147.3 9.6 %collective-permute-start = (bf16[16,1152]{1,0:T(8,128)(2,1)S(1)}, bf16[16,1152]{1,0:T(8,128)(2,1)S(1)}, u32[]{:S(2)}, u32[]{:S(2)}) collective-permute-start(bf16[16,1152]{1,0:T(8,128)(2,1)S(1)} %get-tuple-element.410), channel_id=1, source_target_pairs={{0,16},{16,32},{32,48},{48,64},{64,80},{80,96},{96,112},{112,128},... | collective-permute-start | bytes 110600 | tf_op jit(solution)/shard_map/while/body/eval_jaxpr/ppermute | solution.py:12
  158.1 9.6 %collective-permute-start = (bf16[16,1152]{1,0:T(8,128)(2,1)S(1)}, bf16[16,1152]{1,0:T(8,128)(2,1)S(1)}, u32[]{:S(2)}, u32[]{:S(2)}) collective-permute-start(bf16[16,1152]{1,0:T(8,128)(2,1)S(1)} %get-tuple-element.410), channel_id=1, source_target_pairs={{0,16},{16,32},{32,48},{48,64},{64,80},{80,96},{96,112},{112,128},... | collective-permute-start | bytes 110600 | tf_op jit(solution)/shard_map/while/body/eval_jaxpr/ppermute | solution.py:12
  168.9 9.6 %collective-permute-start = (bf16[16,1152]{1,0:T(8,128)(2,1)S(1)}, bf16[16,1152]{1,0:T(8,128)(2,1)S(1)}, u32[]{:S(2)}, u32[]{:S(2)}) collective-permute-start(bf16[16,1152]{1,0:T(8,128)(2,1)S(1)} %get-tuple-element.410), channel_id=1, source_target_pairs={{0,16},{16,32},{32,48},{48,64},{64,80},{80,96},{96,112},{112,128},... | collective-permute-start | bytes 110600 | tf_op jit(solution)/shard_map/while/body/eval_jaxpr/ppermute | solution.py:12
  179.7 9.6 %collective-permute-start = (bf16[16,1152]{1,0:T(8,128)(2,1)S(1)}, bf16[16,1152]{1,0:T(8,128)(2,1)S(1)}, u32[]{:S(2)}, u32[]{:S(2)}) collective-permute-start(bf16[16,1152]{1,0:T(8,128)(2,1)S(1)} %get-tuple-element.410), channel_id=1, source_target_pairs={{0,16},{16,32},{32,48},{48,64},{64,80},{80,96},{96,112},{112,128},... | collective-permute-start | bytes 110600 | tf_op jit(solution)/shard_map/while/body/eval_jaxpr/ppermute | solution.py:12
  190.5 10.3 %collective-permute-start = (bf16[16,1152]{1,0:T(8,128)(2,1)S(1)}, bf16[16,1152]{1,0:T(8,128)(2,1)S(1)}, u32[]{:S(2)}, u32[]{:S(2)}) collective-permute-start(bf16[16,1152]{1,0:T(8,128)(2,1)S(1)} %get-tuple-element.410), channel_id=1, source_target_pairs={{0,16},{16,32},{32,48},{48,64},{64,80},{80,96},{96,112},{112,128},... | collective-permute-start | bytes 110600 | tf_op jit(solution)/shard_map/while/body/eval_jaxpr/ppermute | solution.py:12
  202.0 10.4 %collective-permute-start = (bf16[16,1152]{1,0:T(8,128)(2,1)S(1)}, bf16[16,1152]{1,0:T(8,128)(2,1)S(1)}, u32[]{:S(2)}, u32[]{:S(2)}) collective-permute-start(bf16[16,1152]{1,0:T(8,128)(2,1)S(1)} %get-tuple-element.410), channel_id=1, source_target_pairs={{0,16},{16,32},{32,48},{48,64},{64,80},{80,96},{96,112},{112,128},... | collective-permute-start | bytes 110600 | tf_op jit(solution)/shard_map/while/body/eval_jaxpr/ppermute | solution.py:12
  204.6 8.8 %collective-permute-start.1 = (f32[16,1152]{1,0:T(8,128)S(1)}, f32[16,1152]{1,0:T(8,128)S(1)}, u32[]{:S(2)}, u32[]{:S(2)}) collective-permute-start(f32[16,1152]{1,0:T(8,128)S(1)} %get-tuple-element.411), channel_id=1, source_target_pairs={{0,16},{16,32},{32,48},{48,64},{64,80},{80,96},{96,112},{112,128},... | collective-permute-start | bytes 221192 | tf_op jit(solution)/shard_map/while/body/eval_jaxpr/ppermute | solution.py:12
  213.6 9.6 %collective-permute-start = (bf16[16,1152]{1,0:T(8,128)(2,1)S(1)}, bf16[16,1152]{1,0:T(8,128)(2,1)S(1)}, u32[]{:S(2)}, u32[]{:S(2)}) collective-permute-start(bf16[16,1152]{1,0:T(8,128)(2,1)S(1)} %get-tuple-element.410), channel_id=1, source_target_pairs={{0,16},{16,32},{32,48},{48,64},{64,80},{80,96},{96,112},{112,128},... | collective-permute-start | bytes 110600 | tf_op jit(solution)/shard_map/while/body/eval_jaxpr/ppermute | solution.py:12
  224.7 9.5 %collective-permute-start = (bf16[16,1152]{1,0:T(8,128)(2,1)S(1)}, bf16[16,1152]{1,0:T(8,128)(2,1)S(1)}, u32[]{:S(2)}, u32[]{:S(2)}) collective-permute-start(bf16[16,1152]{1,0:T(8,128)(2,1)S(1)} %get-tuple-element.410), channel_id=1, source_target_pairs={{0,16},{16,32},{32,48},{48,64},{64,80},{80,96},{96,112},{112,128},... | collective-permute-start | bytes 110600 | tf_op jit(solution)/shard_map/while/body/eval_jaxpr/ppermute | solution.py:12
  227.0 9.5 %collective-permute-start.1 = (f32[16,1152]{1,0:T(8,128)S(1)}, f32[16,1152]{1,0:T(8,128)S(1)}, u32[]{:S(2)}, u32[]{:S(2)}) collective-permute-start(f32[16,1152]{1,0:T(8,128)S(1)} %get-tuple-element.411), channel_id=1, source_target_pairs={{0,16},{16,32},{32,48},{48,64},{64,80},{80,96},{96,112},{112,128},... | collective-permute-start | bytes 221192 | tf_op jit(solution)/shard_map/while/body/eval_jaxpr/ppermute | solution.py:12
  236.7 9.5 %collective-permute-start = (bf16[16,1152]{1,0:T(8,128)(2,1)S(1)}, bf16[16,1152]{1,0:T(8,128)(2,1)S(1)}, u32[]{:S(2)}, u32[]{:S(2)}) collective-permute-start(bf16[16,1152]{1,0:T(8,128)(2,1)S(1)} %get-tuple-element.410), channel_id=1, source_target_pairs={{0,16},{16,32},{32,48},{48,64},{64,80},{80,96},{96,112},{112,128},... | collective-permute-start | bytes 110600 | tf_op jit(solution)/shard_map/while/body/eval_jaxpr/ppermute | solution.py:12
  238.6 9.9 %collective-permute-start.1 = (f32[16,1152]{1,0:T(8,128)S(1)}, f32[16,1152]{1,0:T(8,128)S(1)}, u32[]{:S(2)}, u32[]{:S(2)}) collective-permute-start(f32[16,1152]{1,0:T(8,128)S(1)} %get-tuple-element.411), channel_id=1, source_target_pairs={{0,16},{16,32},{32,48},{48,64},{64,80},{80,96},{96,112},{112,128},... | collective-permute-start | bytes 221192 | tf_op jit(solution)/shard_map/while/body/eval_jaxpr/ppermute | solution.py:12
  248.7 9.5 %collective-permute-start = (bf16[16,1152]{1,0:T(8,128)(2,1)S(1)}, bf16[16,1152]{1,0:T(8,128)(2,1)S(1)}, u32[]{:S(2)}, u32[]{:S(2)}) collective-permute-start(bf16[16,1152]{1,0:T(8,128)(2,1)S(1)} %get-tuple-element.410), channel_id=1, source_target_pairs={{0,16},{16,32},{32,48},{48,64},{64,80},{80,96},{96,112},{112,128},... | collective-permute-start | bytes 110600 | tf_op jit(solution)/shard_map/while/body/eval_jaxpr/ppermute | solution.py:12
  250.7 9.9 %collective-permute-start.1 = (f32[16,1152]{1,0:T(8,128)S(1)}, f32[16,1152]{1,0:T(8,128)S(1)}, u32[]{:S(2)}, u32[]{:S(2)}) collective-permute-start(f32[16,1152]{1,0:T(8,128)S(1)} %get-tuple-element.411), channel_id=1, source_target_pairs={{0,16},{16,32},{32,48},{48,64},{64,80},{80,96},{96,112},{112,128},... | collective-permute-start | bytes 221192 | tf_op jit(solution)/shard_map/while/body/eval_jaxpr/ppermute | solution.py:12
  260.8 9.5 %collective-permute-start = (bf16[16,1152]{1,0:T(8,128)(2,1)S(1)}, bf16[16,1152]{1,0:T(8,128)(2,1)S(1)}, u32[]{:S(2)}, u32[]{:S(2)}) collective-permute-start(bf16[16,1152]{1,0:T(8,128)(2,1)S(1)} %get-tuple-element.410), channel_id=1, source_target_pairs={{0,16},{16,32},{32,48},{48,64},{64,80},{80,96},{96,112},{112,128},... | collective-permute-start | bytes 110600 | tf_op jit(solution)/shard_map/while/body/eval_jaxpr/ppermute | solution.py:12
  262.7 9.9 %collective-permute-start.1 = (f32[16,1152]{1,0:T(8,128)S(1)}, f32[16,1152]{1,0:T(8,128)S(1)}, u32[]{:S(2)}, u32[]{:S(2)}) collective-permute-start(f32[16,1152]{1,0:T(8,128)S(1)} %get-tuple-element.411), channel_id=1, source_target_pairs={{0,16},{16,32},{32,48},{48,64},{64,80},{80,96},{96,112},{112,128},... | collective-permute-start | bytes 221192 | tf_op jit(solution)/shard_map/while/body/eval_jaxpr/ppermute | solution.py:12
  272.8 9.5 %collective-permute-start = (bf16[16,1152]{1,0:T(8,128)(2,1)S(1)}, bf16[16,1152]{1,0:T(8,128)(2,1)S(1)}, u32[]{:S(2)}, u32[]{:S(2)}) collective-permute-start(bf16[16,1152]{1,0:T(8,128)(2,1)S(1)} %get-tuple-element.410), channel_id=1, source_target_pairs={{0,16},{16,32},{32,48},{48,64},{64,80},{80,96},{96,112},{112,128},... | collective-permute-start | bytes 110600 | tf_op jit(solution)/shard_map/while/body/eval_jaxpr/ppermute | solution.py:12
  274.7 9.9 %collective-permute-start.1 = (f32[16,1152]{1,0:T(8,128)S(1)}, f32[16,1152]{1,0:T(8,128)S(1)}, u32[]{:S(2)}, u32[]{:S(2)}) collective-permute-start(f32[16,1152]{1,0:T(8,128)S(1)} %get-tuple-element.411), channel_id=1, source_target_pairs={{0,16},{16,32},{32,48},{48,64},{64,80},{80,96},{96,112},{112,128},... | collective-permute-start | bytes 221192 | tf_op jit(solution)/shard_map/while/body/eval_jaxpr/ppermute | solution.py:12
  284.8 9.5 %collective-permute-start = (bf16[16,1152]{1,0:T(8,128)(2,1)S(1)}, bf16[16,1152]{1,0:T(8,128)(2,1)S(1)}, u32[]{:S(2)}, u32[]{:S(2)}) collective-permute-start(bf16[16,1152]{1,0:T(8,128)(2,1)S(1)} %get-tuple-element.410), channel_id=1, source_target_pairs={{0,16},{16,32},{32,48},{48,64},{64,80},{80,96},{96,112},{112,128},... | collective-permute-start | bytes 110600 | tf_op jit(solution)/shard_map/while/body/eval_jaxpr/ppermute | solution.py:12
  286.8 9.9 %collective-permute-start.1 = (f32[16,1152]{1,0:T(8,128)S(1)}, f32[16,1152]{1,0:T(8,128)S(1)}, u32[]{:S(2)}, u32[]{:S(2)}) collective-permute-start(f32[16,1152]{1,0:T(8,128)S(1)} %get-tuple-element.411), channel_id=1, source_target_pairs={{0,16},{16,32},{32,48},{48,64},{64,80},{80,96},{96,112},{112,128},... | collective-permute-start | bytes 221192 | tf_op jit(solution)/shard_map/while/body/eval_jaxpr/ppermute | solution.py:12
  296.9 9.5 %collective-permute-start = (bf16[16,1152]{1,0:T(8,128)(2,1)S(1)}, bf16[16,1152]{1,0:T(8,128)(2,1)S(1)}, u32[]{:S(2)}, u32[]{:S(2)}) collective-permute-start(bf16[16,1152]{1,0:T(8,128)(2,1)S(1)} %get-tuple-element.410), channel_id=1, source_target_pairs={{0,16},{16,32},{32,48},{48,64},{64,80},{80,96},{96,112},{112,128},... | collective-permute-start | bytes 110600 | tf_op jit(solution)/shard_map/while/body/eval_jaxpr/ppermute | solution.py:12
  298.8 9.9 %collective-permute-start.1 = (f32[16,1152]{1,0:T(8,128)S(1)}, f32[16,1152]{1,0:T(8,128)S(1)}, u32[]{:S(2)}, u32[]{:S(2)}) collective-permute-start(f32[16,1152]{1,0:T(8,128)S(1)} %get-tuple-element.411), channel_id=1, source_target_pairs={{0,16},{16,32},{32,48},{48,64},{64,80},{80,96},{96,112},{112,128},... | collective-permute-start | bytes 221192 | tf_op jit(solution)/shard_map/while/body/eval_jaxpr/ppermute | solution.py:12
  308.9 9.8 %collective-permute-start = (bf16[16,1152]{1,0:T(8,128)(2,1)S(1)}, bf16[16,1152]{1,0:T(8,128)(2,1)S(1)}, u32[]{:S(2)}, u32[]{:S(2)}) collective-permute-start(bf16[16,1152]{1,0:T(8,128)(2,1)S(1)} %get-tuple-element.410), channel_id=1, source_target_pairs={{0,16},{16,32},{32,48},{48,64},{64,80},{80,96},{96,112},{112,128},... | collective-permute-start | bytes 110600 | tf_op jit(solution)/shard_map/while/body/eval_jaxpr/ppermute | solution.py:12
  310.8 10.2 %collective-permute-start.1 = (f32[16,1152]{1,0:T(8,128)S(1)}, f32[16,1152]{1,0:T(8,128)S(1)}, u32[]{:S(2)}, u32[]{:S(2)}) collective-permute-start(f32[16,1152]{1,0:T(8,128)S(1)} %get-tuple-element.411), channel_id=1, source_target_pairs={{0,16},{16,32},{32,48},{48,64},{64,80},{80,96},{96,112},{112,128},... | collective-permute-start | bytes 221192 | tf_op jit(solution)/shard_map/while/body/eval_jaxpr/ppermute | solution.py:12
  321.2 9.5 %collective-permute-start = (bf16[16,1152]{1,0:T(8,128)(2,1)S(1)}, bf16[16,1152]{1,0:T(8,128)(2,1)S(1)}, u32[]{:S(2)}, u32[]{:S(2)}) collective-permute-start(bf16[16,1152]{1,0:T(8,128)(2,1)S(1)} %get-tuple-element.410), channel_id=1, source_target_pairs={{0,16},{16,32},{32,48},{48,64},{64,80},{80,96},{96,112},{112,128},... | collective-permute-start | bytes 110600 | tf_op jit(solution)/shard_map/while/body/eval_jaxpr/ppermute | solution.py:12
  323.1 9.9 %collective-permute-start.1 = (f32[16,1152]{1,0:T(8,128)S(1)}, f32[16,1152]{1,0:T(8,128)S(1)}, u32[]{:S(2)}, u32[]{:S(2)}) collective-permute-start(f32[16,1152]{1,0:T(8,128)S(1)} %get-tuple-element.411), channel_id=1, source_target_pairs={{0,16},{16,32},{32,48},{48,64},{64,80},{80,96},{96,112},{112,128},... | collective-permute-start | bytes 221192 | tf_op jit(solution)/shard_map/while/body/eval_jaxpr/ppermute | solution.py:12
  333.3 9.5 %collective-permute-start = (bf16[16,1152]{1,0:T(8,128)(2,1)S(1)}, bf16[16,1152]{1,0:T(8,128)(2,1)S(1)}, u32[]{:S(2)}, u32[]{:S(2)}) collective-permute-start(bf16[16,1152]{1,0:T(8,128)(2,1)S(1)} %get-tuple-element.410), channel_id=1, source_target_pairs={{0,16},{16,32},{32,48},{48,64},{64,80},{80,96},{96,112},{112,128},... | collective-permute-start | bytes 110600 | tf_op jit(solution)/shard_map/while/body/eval_jaxpr/ppermute | solution.py:12
  335.2 9.9 %collective-permute-start.1 = (f32[16,1152]{1,0:T(8,128)S(1)}, f32[16,1152]{1,0:T(8,128)S(1)}, u32[]{:S(2)}, u32[]{:S(2)}) collective-permute-start(f32[16,1152]{1,0:T(8,128)S(1)} %get-tuple-element.411), channel_id=1, source_target_pairs={{0,16},{16,32},{32,48},{48,64},{64,80},{80,96},{96,112},{112,128},... | collective-permute-start | bytes 221192 | tf_op jit(solution)/shard_map/while/body/eval_jaxpr/ppermute | solution.py:12
  345.3 9.5 %collective-permute-start = (bf16[16,1152]{1,0:T(8,128)(2,1)S(1)}, bf16[16,1152]{1,0:T(8,128)(2,1)S(1)}, u32[]{:S(2)}, u32[]{:S(2)}) collective-permute-start(bf16[16,1152]{1,0:T(8,128)(2,1)S(1)} %get-tuple-element.410), channel_id=1, source_target_pairs={{0,16},{16,32},{32,48},{48,64},{64,80},{80,96},{96,112},{112,128},... | collective-permute-start | bytes 110600 | tf_op jit(solution)/shard_map/while/body/eval_jaxpr/ppermute | solution.py:12
  347.2 9.9 %collective-permute-start.1 = (f32[16,1152]{1,0:T(8,128)S(1)}, f32[16,1152]{1,0:T(8,128)S(1)}, u32[]{:S(2)}, u32[]{:S(2)}) collective-permute-start(f32[16,1152]{1,0:T(8,128)S(1)} %get-tuple-element.411), channel_id=1, source_target_pairs={{0,16},{16,32},{32,48},{48,64},{64,80},{80,96},{96,112},{112,128},... | collective-permute-start | bytes 221192 | tf_op jit(solution)/shard_map/while/body/eval_jaxpr/ppermute | solution.py:12
  357.3 9.7 %collective-permute-start = (bf16[16,1152]{1,0:T(8,128)(2,1)S(1)}, bf16[16,1152]{1,0:T(8,128)(2,1)S(1)}, u32[]{:S(2)}, u32[]{:S(2)}) collective-permute-start(bf16[16,1152]{1,0:T(8,128)(2,1)S(1)} %get-tuple-element.410), channel_id=1, source_target_pairs={{0,16},{16,32},{32,48},{48,64},{64,80},{80,96},{96,112},{112,128},... | collective-permute-start | bytes 110600 | tf_op jit(solution)/shard_map/while/body/eval_jaxpr/ppermute | solution.py:12
  359.2 10.1 %collective-permute-start.1 = (f32[16,1152]{1,0:T(8,128)S(1)}, f32[16,1152]{1,0:T(8,128)S(1)}, u32[]{:S(2)}, u32[]{:S(2)}) collective-permute-start(f32[16,1152]{1,0:T(8,128)S(1)} %get-tuple-element.411), channel_id=1, source_target_pairs={{0,16},{16,32},{32,48},{48,64},{64,80},{80,96},{96,112},{112,128},... | collective-permute-start | bytes 221192 | tf_op jit(solution)/shard_map/while/body/eval_jaxpr/ppermute | solution.py:12
  369.6 9.6 %collective-permute-start = (bf16[16,1152]{1,0:T(8,128)(2,1)S(1)}, bf16[16,1152]{1,0:T(8,128)(2,1)S(1)}, u32[]{:S(2)}, u32[]{:S(2)}) collective-permute-start(bf16[16,1152]{1,0:T(8,128)(2,1)S(1)} %get-tuple-element.410), channel_id=1, source_target_pairs={{0,16},{16,32},{32,48},{48,64},{64,80},{80,96},{96,112},{112,128},... | collective-permute-start | bytes 110600 | tf_op jit(solution)/shard_map/while/body/eval_jaxpr/ppermute | solution.py:12
  371.5 10.0 %collective-permute-start.1 = (f32[16,1152]{1,0:T(8,128)S(1)}, f32[16,1152]{1,0:T(8,128)S(1)}, u32[]{:S(2)}, u32[]{:S(2)}) collective-permute-start(f32[16,1152]{1,0:T(8,128)S(1)} %get-tuple-element.411), channel_id=1, source_target_pairs={{0,16},{16,32},{32,48},{48,64},{64,80},{80,96},{96,112},{112,128},... | collective-permute-start | bytes 221192 | tf_op jit(solution)/shard_map/while/body/eval_jaxpr/ppermute | solution.py:12
  381.7 9.5 %collective-permute-start = (bf16[16,1152]{1,0:T(8,128)(2,1)S(1)}, bf16[16,1152]{1,0:T(8,128)(2,1)S(1)}, u32[]{:S(2)}, u32[]{:S(2)}) collective-permute-start(bf16[16,1152]{1,0:T(8,128)(2,1)S(1)} %get-tuple-element.410), channel_id=1, source_target_pairs={{0,16},{16,32},{32,48},{48,64},{64,80},{80,96},{96,112},{112,128},... | collective-permute-start | bytes 110600 | tf_op jit(solution)/shard_map/while/body/eval_jaxpr/ppermute | solution.py:12
  383.6 9.9 %collective-permute-start.1 = (f32[16,1152]{1,0:T(8,128)S(1)}, f32[16,1152]{1,0:T(8,128)S(1)}, u32[]{:S(2)}, u32[]{:S(2)}) collective-permute-start(f32[16,1152]{1,0:T(8,128)S(1)} %get-tuple-element.411), channel_id=1, source_target_pairs={{0,16},{16,32},{32,48},{48,64},{64,80},{80,96},{96,112},{112,128},... | collective-permute-start | bytes 221192 | tf_op jit(solution)/shard_map/while/body/eval_jaxpr/ppermute | solution.py:12
  393.7 9.5 %collective-permute-start = (bf16[16,1152]{1,0:T(8,128)(2,1)S(1)}, bf16[16,1152]{1,0:T(8,128)(2,1)S(1)}, u32[]{:S(2)}, u32[]{:S(2)}) collective-permute-start(bf16[16,1152]{1,0:T(8,128)(2,1)S(1)} %get-tuple-element.410), channel_id=1, source_target_pairs={{0,16},{16,32},{32,48},{48,64},{64,80},{80,96},{96,112},{112,128},... | collective-permute-start | bytes 110600 | tf_op jit(solution)/shard_map/while/body/eval_jaxpr/ppermute | solution.py:12
  395.6 9.9 %collective-permute-start.1 = (f32[16,1152]{1,0:T(8,128)S(1)}, f32[16,1152]{1,0:T(8,128)S(1)}, u32[]{:S(2)}, u32[]{:S(2)}) collective-permute-start(f32[16,1152]{1,0:T(8,128)S(1)} %get-tuple-element.411), channel_id=1, source_target_pairs={{0,16},{16,32},{32,48},{48,64},{64,80},{80,96},{96,112},{112,128},... | collective-permute-start | bytes 221192 | tf_op jit(solution)/shard_map/while/body/eval_jaxpr/ppermute | solution.py:12
  407.3 10.0 %collective-permute-start.2 = (f32[16,1152]{1,0:T(8,128)S(1)}, f32[16,1152]{1,0:T(8,128)S(1)}, u32[]{:S(2)}, u32[]{:S(2)}) collective-permute-start(f32[16,1152]{1,0:T(8,128)S(1)} %get-tuple-element.271), channel_id=1, source_target_pairs={{0,16},{16,32},{32,48},{48,64},{64,80},{80,96},{96,112},{112,128},... | collective-permute-start | bytes 221192 | tf_op jit(solution)/shard_map/ppermute | solution.py:12
  (18 other events, 223.2 us)
Sparse Core Ops, SparseCore 0:
  407.4 94.3 reduce-scatter.1
where the time goes:
time: 514 us; the launch traced here: 511 us
  starting transfers between devices  234 us (46%)
  waiting for transfers between devices  170 us (33%)
  blocking collectives  42.7 us (8%)
  matrix products  37.2 us (7%)
  between operations  15.4 us (3%)
  other arithmetic  7.44 us (1%)
    ppermute x63, starting transfers between devices, from_behind(): return lax.ppermute(value, axis, pairs)  234 us
    ppermute x63, waiting for transfers between devices, from_behind(): return lax.ppermute(value, axis, pairs)  86.4 us
    reduce_scatter x1, waiting for transfers between devices, per_device(): lax.psum_scatter(image_terms, 'grp', scatter_dimension=0, tiled=True)  83.5 us
    all_gather x1, blocking collectives, per_device(): lax.all_gather(img_unit.astype(jnp.bfloat16), 'grp', axis=0, tiled=True)  42.7 us
    dot_general x32, matrix products, station(): jnp.einsum('id,kd->ik', image_block, moving, preferred_element_type=jnp.f...  29.5 us
  transfers between devices with their start and end apart: 64, of which 37 were waited for; matrix products, arithmetic and copies ran while one was open for 6% of the time, Pallas kernels for 0%

commit v1 on v0

--- a/solution.py
+++ b/solution.py
@@ -41,7 +41,12 @@
     offset = bias[0]
     img_unit, img_length = normalize(image_emb)
     txt_unit, txt_length = normalize(text_emb)
-    image_block = lax.all_gather(img_unit.astype(jnp.bfloat16), "grp", axis=0, tiled=True)
+    image_block = jnp.concatenate(
+        lax.all_to_all(
+            jnp.stack([img_unit.astype(jnp.bfloat16)] * lax.axis_size("grp")), "grp", 0, 0
+        ),
+        axis=0,
+    )
     block_rows = groups * row_count
     image_ids = loop_at * block_rows + jnp.arange(block_rows, dtype=jnp.int32)
     text_rows = txt_unit.astype(jnp.bfloat16)

time: 514 us -> 499 us (0.971)
  the two profiles are of different devices: /device:TPU:4 before, /device:TPU:6 now
where the time goes in v1:
time: 499 us; the launch traced here: 497 us
  starting transfers between devices  325 us (65%)
  waiting for transfers between devices  107 us (21%)
  matrix products  37.3 us (7%)
  between operations  15.5 us (3%)
  other arithmetic  5.92 us (1%)
    ppermute x63, starting transfers between devices, from_behind(): return lax.ppermute(value, axis, pairs)  314 us
    reduce_scatter x1, waiting for transfers between devices, per_device(): lax.psum_scatter(image_terms, 'grp', scatter_dimension=0, tiled=True)  89.8 us
    dot_general x32, matrix products, station(): jnp.einsum('id,kd->ik', image_block, moving, preferred_element_type=jnp.f...  29.5 us
    all_to_all x1, waiting for transfers between devices, per_device(): lax.all_to_all(jnp.stack([img_unit.astype(jnp.bfloat16)] * lax.axis_size(...  14.9 us
    all_to_all x1, starting transfers between devices, per_device(): lax.all_to_all(jnp.stack([img_unit.astype(jnp.bfloat16)] * lax.axis_size(...  11.4 us
  transfers between devices with their start and end apart: 65, of which 4 were waited for; matrix products, arithmetic and copies ran while one was open for 6% of the time, Pallas kernels for 0%

profile of v1, /device:TPU:6, one launch (start us, length us, event | category | flops | bytes accessed | tf_op | source)
XLA Modules:
  0.0 496.5 jit_solution(949967155378385466)
XLA Ops:
  9.8 11.4 %all-to-all-start = ((bf16[16,16,1152]{2,1,0:T(8,128)(2,1)}), bf16[16,16,1152]{2,1,0:T(8,128)(2,1)S(1)}, u32[]{:S(2)}, u32[]{:S(2)}) async-start(bf16[16,16,1152]{2,1,0:T(8,128)(2,1)} %stack.2), calls=%async_computation | async-start | bytes 1179648 | tf_op jit(solution)/shard_map/all_to_all | solution.py:45
  23.0 14.9 %all-to-all-done = bf16[16,16,1152]{2,1,0:T(8,128)(2,1)S(1)} async-done(((bf16[16,16,1152]{2,1,0:T(8,128)(2,1)}), bf16[16,16,1152]{2,1,0:T(8,128)(2,1)S(1)}, u32[]{:S(2)}, u32[]{:S(2)}) %all-to-all-start) | async-done | bytes 589856 | tf_op jit(solution)/shard_map/all_to_all | solution.py:45
  38.5 350.6 %while.22 = (s32[]{:T(128)}, bf16[16,1152]{1,0:T(8,128)(2,1)S(1)}, f32[16,1152]{1,0:T(8,128)S(1)}, bf16[256,512]{0,1:T(8,128)(2,1)S(1)}, bf16[512,1152]{1,0:T(8,...) while((s32[]{:T(128)}, bf16[16,1152]{1,0:T(8,128)(2,1)S(1)}, ...), condition=%wide.region_3.4_spmd.clone, body=%wide.region_2.3_spmd.clone.sunk | while | flops 18934052 | bytes 1981456 | solution.py:87
  40.4 4.5 collective-permute-start.1
  48.4 7.4 %collective-permute-start.1 = (f32[16,1152]{1,0:T(8,128)S(1)}, f32[16,1152]{1,0:T(8,128)S(1)}, u32[]{:S(2)}, u32[]{:S(2)}) collective-permute-start(f32[16,1152]{1,0:T(8,128)S(1)} %get-tuple-element.411), channel_id=1, source_target_pairs={{0,16},{16,32},{32,48},{48,64},{64,80},{80,96},{96,112},{112,128},... | collective-permute-start | bytes 221192 | tf_op jit(solution)/shard_map/while/body/eval_jaxpr/ppermute | solution.py:12
  59.4 7.3 %collective-permute-start.1 = (f32[16,1152]{1,0:T(8,128)S(1)}, f32[16,1152]{1,0:T(8,128)S(1)}, u32[]{:S(2)}, u32[]{:S(2)}) collective-permute-start(f32[16,1152]{1,0:T(8,128)S(1)} %get-tuple-element.411), channel_id=1, source_target_pairs={{0,16},{16,32},{32,48},{48,64},{64,80},{80,96},{96,112},{112,128},... | collective-permute-start | bytes 221192 | tf_op jit(solution)/shard_map/while/body/eval_jaxpr/ppermute | solution.py:12
  70.2 7.3 %collective-permute-start.1 = (f32[16,1152]{1,0:T(8,128)S(1)}, f32[16,1152]{1,0:T(8,128)S(1)}, u32[]{:S(2)}, u32[]{:S(2)}) collective-permute-start(f32[16,1152]{1,0:T(8,128)S(1)} %get-tuple-element.411), channel_id=1, source_target_pairs={{0,16},{16,32},{32,48},{48,64},{64,80},{80,96},{96,112},{112,128},... | collective-permute-start | bytes 221192 | tf_op jit(solution)/shard_map/while/body/eval_jaxpr/ppermute | solution.py:12
  81.0 7.3 %collective-permute-start.1 = (f32[16,1152]{1,0:T(8,128)S(1)}, f32[16,1152]{1,0:T(8,128)S(1)}, u32[]{:S(2)}, u32[]{:S(2)}) collective-permute-start(f32[16,1152]{1,0:T(8,128)S(1)} %get-tuple-element.411), channel_id=1, source_target_pairs={{0,16},{16,32},{32,48},{48,64},{64,80},{80,96},{96,112},{112,128},... | collective-permute-start | bytes 221192 | tf_op jit(solution)/shard_map/while/body/eval_jaxpr/ppermute | solution.py:12
  91.8 7.3 %collective-permute-start.1 = (f32[16,1152]{1,0:T(8,128)S(1)}, f32[16,1152]{1,0:T(8,128)S(1)}, u32[]{:S(2)}, u32[]{:S(2)}) collective-permute-start(f32[16,1152]{1,0:T(8,128)S(1)} %get-tuple-element.411), channel_id=1, source_target_pairs={{0,16},{16,32},{32,48},{48,64},{64,80},{80,96},{96,112},{112,128},... | collective-permute-start | bytes 221192 | tf_op jit(solution)/shard_map/while/body/eval_jaxpr/ppermute | solution.py:12
  102.7 7.3 %collective-permute-start.1 = (f32[16,1152]{1,0:T(8,128)S(1)}, f32[16,1152]{1,0:T(8,128)S(1)}, u32[]{:S(2)}, u32[]{:S(2)}) collective-permute-start(f32[16,1152]{1,0:T(8,128)S(1)} %get-tuple-element.411), channel_id=1, source_target_pairs={{0,16},{16,32},{32,48},{48,64},{64,80},{80,96},{96,112},{112,128},... | collective-permute-start | bytes 221192 | tf_op jit(solution)/shard_map/while/body/eval_jaxpr/ppermute | solution.py:12
  113.5 7.3 %collective-permute-start.1 = (f32[16,1152]{1,0:T(8,128)S(1)}, f32[16,1152]{1,0:T(8,128)S(1)}, u32[]{:S(2)}, u32[]{:S(2)}) collective-permute-start(f32[16,1152]{1,0:T(8,128)S(1)} %get-tuple-element.411), channel_id=1, source_target_pairs={{0,16},{16,32},{32,48},{48,64},{64,80},{80,96},{96,112},{112,128},... | collective-permute-start | bytes 221192 | tf_op jit(solution)/shard_map/while/body/eval_jaxpr/ppermute | solution.py:12
  124.3 7.3 %collective-permute-start.1 = (f32[16,1152]{1,0:T(8,128)S(1)}, f32[16,1152]{1,0:T(8,128)S(1)}, u32[]{:S(2)}, u32[]{:S(2)}) collective-permute-start(f32[16,1152]{1,0:T(8,128)S(1)} %get-tuple-element.411), channel_id=1, source_target_pairs={{0,16},{16,32},{32,48},{48,64},{64,80},{80,96},{96,112},{112,128},... | collective-permute-start | bytes 221192 | tf_op jit(solution)/shard_map/while/body/eval_jaxpr/ppermute | solution.py:12
  135.8 7.5 %collective-permute-start.1 = (f32[16,1152]{1,0:T(8,128)S(1)}, f32[16,1152]{1,0:T(8,128)S(1)}, u32[]{:S(2)}, u32[]{:S(2)}) collective-permute-start(f32[16,1152]{1,0:T(8,128)S(1)} %get-tuple-element.411), channel_id=1, source_target_pairs={{0,16},{16,32},{32,48},{48,64},{64,80},{80,96},{96,112},{112,128},... | collective-permute-start | bytes 221192 | tf_op jit(solution)/shard_map/while/body/eval_jaxpr/ppermute | solution.py:12
  146.8 7.3 %collective-permute-start.1 = (f32[16,1152]{1,0:T(8,128)S(1)}, f32[16,1152]{1,0:T(8,128)S(1)}, u32[]{:S(2)}, u32[]{:S(2)}) collective-permute-start(f32[16,1152]{1,0:T(8,128)S(1)} %get-tuple-element.411), channel_id=1, source_target_pairs={{0,16},{16,32},{32,48},{48,64},{64,80},{80,96},{96,112},{112,128},... | collective-permute-start | bytes 221192 | tf_op jit(solution)/shard_map/while/body/eval_jaxpr/ppermute | solution.py:12
  158.0 7.4 %collective-permute-start.1 = (f32[16,1152]{1,0:T(8,128)S(1)}, f32[16,1152]{1,0:T(8,128)S(1)}, u32[]{:S(2)}, u32[]{:S(2)}) collective-permute-start(f32[16,1152]{1,0:T(8,128)S(1)} %get-tuple-element.411), channel_id=1, source_target_pairs={{0,16},{16,32},{32,48},{48,64},{64,80},{80,96},{96,112},{112,128},... | collective-permute-start | bytes 221192 | tf_op jit(solution)/shard_map/while/body/eval_jaxpr/ppermute | solution.py:12
  168.9 7.3 %collective-permute-start.1 = (f32[16,1152]{1,0:T(8,128)S(1)}, f32[16,1152]{1,0:T(8,128)S(1)}, u32[]{:S(2)}, u32[]{:S(2)}) collective-permute-start(f32[16,1152]{1,0:T(8,128)S(1)} %get-tuple-element.411), channel_id=1, source_target_pairs={{0,16},{16,32},{32,48},{48,64},{64,80},{80,96},{96,112},{112,128},... | collective-permute-start | bytes 221192 | tf_op jit(solution)/shard_map/while/body/eval_jaxpr/ppermute | solution.py:12
  179.8 7.3 %collective-permute-start.1 = (f32[16,1152]{1,0:T(8,128)S(1)}, f32[16,1152]{1,0:T(8,128)S(1)}, u32[]{:S(2)}, u32[]{:S(2)}) collective-permute-start(f32[16,1152]{1,0:T(8,128)S(1)} %get-tuple-element.411), channel_id=1, source_target_pairs={{0,16},{16,32},{32,48},{48,64},{64,80},{80,96},{96,112},{112,128},... | collective-permute-start | bytes 221192 | tf_op jit(solution)/shard_map/while/body/eval_jaxpr/ppermute | solution.py:12
  190.6 7.3 %collective-permute-start.1 = (f32[16,1152]{1,0:T(8,128)S(1)}, f32[16,1152]{1,0:T(8,128)S(1)}, u32[]{:S(2)}, u32[]{:S(2)}) collective-permute-start(f32[16,1152]{1,0:T(8,128)S(1)} %get-tuple-element.411), channel_id=1, source_target_pairs={{0,16},{16,32},{32,48},{48,64},{64,80},{80,96},{96,112},{112,128},... | collective-permute-start | bytes 221192 | tf_op jit(solution)/shard_map/while/body/eval_jaxpr/ppermute | solution.py:12
  201.4 7.3 %collective-permute-start.1 = (f32[16,1152]{1,0:T(8,128)S(1)}, f32[16,1152]{1,0:T(8,128)S(1)}, u32[]{:S(2)}, u32[]{:S(2)}) collective-permute-start(f32[16,1152]{1,0:T(8,128)S(1)} %get-tuple-element.411), channel_id=1, source_target_pairs={{0,16},{16,32},{32,48},{48,64},{64,80},{80,96},{96,112},{112,128},... | collective-permute-start | bytes 221192 | tf_op jit(solution)/shard_map/while/body/eval_jaxpr/ppermute | solution.py:12
  212.2 7.3 %collective-permute-start.1 = (f32[16,1152]{1,0:T(8,128)S(1)}, f32[16,1152]{1,0:T(8,128)S(1)}, u32[]{:S(2)}, u32[]{:S(2)}) collective-permute-start(f32[16,1152]{1,0:T(8,128)S(1)} %get-tuple-element.411), channel_id=1, source_target_pairs={{0,16},{16,32},{32,48},{48,64},{64,80},{80,96},{96,112},{112,128},... | collective-permute-start | bytes 221192 | tf_op jit(solution)/shard_map/while/body/eval_jaxpr/ppermute | solution.py:12
  224.1 7.3 %collective-permute-start.1 = (f32[16,1152]{1,0:T(8,128)S(1)}, f32[16,1152]{1,0:T(8,128)S(1)}, u32[]{:S(2)}, u32[]{:S(2)}) collective-permute-start(f32[16,1152]{1,0:T(8,128)S(1)} %get-tuple-element.411), channel_id=1, source_target_pairs={{0,16},{16,32},{32,48},{48,64},{64,80},{80,96},{96,112},{112,128},... | collective-permute-start | bytes 221192 | tf_op jit(solution)/shard_map/while/body/eval_jaxpr/ppermute | solution.py:12
  232.6 3.5 collective-permute-start
  236.1 7.3 %collective-permute-start.1 = (f32[16,1152]{1,0:T(8,128)S(1)}, f32[16,1152]{1,0:T(8,128)S(1)}, u32[]{:S(2)}, u32[]{:S(2)}) collective-permute-start(f32[16,1152]{1,0:T(8,128)S(1)} %get-tuple-element.411), channel_id=1, source_target_pairs={{0,16},{16,32},{32,48},{48,64},{64,80},{80,96},{96,112},{112,128},... | collective-permute-start | bytes 221192 | tf_op jit(solution)/shard_map/while/body/eval_jaxpr/ppermute | solution.py:12
  244.7 3.5 collective-permute-start
  248.1 7.3 %collective-permute-start.1 = (f32[16,1152]{1,0:T(8,128)S(1)}, f32[16,1152]{1,0:T(8,128)S(1)}, u32[]{:S(2)}, u32[]{:S(2)}) collective-permute-start(f32[16,1152]{1,0:T(8,128)S(1)} %get-tuple-element.411), channel_id=1, source_target_pairs={{0,16},{16,32},{32,48},{48,64},{64,80},{80,96},{96,112},{112,128},... | collective-permute-start | bytes 221192 | tf_op jit(solution)/shard_map/while/body/eval_jaxpr/ppermute | solution.py:12
  256.7 3.5 collective-permute-start
  260.1 7.3 %collective-permute-start.1 = (f32[16,1152]{1,0:T(8,128)S(1)}, f32[16,1152]{1,0:T(8,128)S(1)}, u32[]{:S(2)}, u32[]{:S(2)}) collective-permute-start(f32[16,1152]{1,0:T(8,128)S(1)} %get-tuple-element.411), channel_id=1, source_target_pairs={{0,16},{16,32},{32,48},{48,64},{64,80},{80,96},{96,112},{112,128},... | collective-permute-start | bytes 221192 | tf_op jit(solution)/shard_map/while/body/eval_jaxpr/ppermute | solution.py:12
  268.7 3.5 collective-permute-start
  272.2 7.3 %collective-permute-start.1 = (f32[16,1152]{1,0:T(8,128)S(1)}, f32[16,1152]{1,0:T(8,128)S(1)}, u32[]{:S(2)}, u32[]{:S(2)}) collective-permute-start(f32[16,1152]{1,0:T(8,128)S(1)} %get-tuple-element.411), channel_id=1, source_target_pairs={{0,16},{16,32},{32,48},{48,64},{64,80},{80,96},{96,112},{112,128},... | collective-permute-start | bytes 221192 | tf_op jit(solution)/shard_map/while/body/eval_jaxpr/ppermute | solution.py:12
  280.7 3.5 collective-permute-start
  284.2 7.3 %collective-permute-start.1 = (f32[16,1152]{1,0:T(8,128)S(1)}, f32[16,1152]{1,0:T(8,128)S(1)}, u32[]{:S(2)}, u32[]{:S(2)}) collective-permute-start(f32[16,1152]{1,0:T(8,128)S(1)} %get-tuple-element.411), channel_id=1, source_target_pairs={{0,16},{16,32},{32,48},{48,64},{64,80},{80,96},{96,112},{112,128},... | collective-permute-start | bytes 221192 | tf_op jit(solution)/shard_map/while/body/eval_jaxpr/ppermute | solution.py:12
  292.8 3.5 collective-permute-start
  296.2 7.3 %collective-permute-start.1 = (f32[16,1152]{1,0:T(8,128)S(1)}, f32[16,1152]{1,0:T(8,128)S(1)}, u32[]{:S(2)}, u32[]{:S(2)}) collective-permute-start(f32[16,1152]{1,0:T(8,128)S(1)} %get-tuple-element.411), channel_id=1, source_target_pairs={{0,16},{16,32},{32,48},{48,64},{64,80},{80,96},{96,112},{112,128},... | collective-permute-start | bytes 221192 | tf_op jit(solution)/shard_map/while/body/eval_jaxpr/ppermute | solution.py:12
  304.8 3.5 collective-permute-start
  308.3 7.3 %collective-permute-start.1 = (f32[16,1152]{1,0:T(8,128)S(1)}, f32[16,1152]{1,0:T(8,128)S(1)}, u32[]{:S(2)}, u32[]{:S(2)}) collective-permute-start(f32[16,1152]{1,0:T(8,128)S(1)} %get-tuple-element.411), channel_id=1, source_target_pairs={{0,16},{16,32},{32,48},{48,64},{64,80},{80,96},{96,112},{112,128},... | collective-permute-start | bytes 221192 | tf_op jit(solution)/shard_map/while/body/eval_jaxpr/ppermute | solution.py:12
  316.8 3.5 collective-permute-start
  320.3 7.3 %collective-permute-start.1 = (f32[16,1152]{1,0:T(8,128)S(1)}, f32[16,1152]{1,0:T(8,128)S(1)}, u32[]{:S(2)}, u32[]{:S(2)}) collective-permute-start(f32[16,1152]{1,0:T(8,128)S(1)} %get-tuple-element.411), channel_id=1, source_target_pairs={{0,16},{16,32},{32,48},{48,64},{64,80},{80,96},{96,112},{112,128},... | collective-permute-start | bytes 221192 | tf_op jit(solution)/shard_map/while/body/eval_jaxpr/ppermute | solution.py:12
  328.9 3.5 collective-permute-start
  332.3 7.3 %collective-permute-start.1 = (f32[16,1152]{1,0:T(8,128)S(1)}, f32[16,1152]{1,0:T(8,128)S(1)}, u32[]{:S(2)}, u32[]{:S(2)}) collective-permute-start(f32[16,1152]{1,0:T(8,128)S(1)} %get-tuple-element.411), channel_id=1, source_target_pairs={{0,16},{16,32},{32,48},{48,64},{64,80},{80,96},{96,112},{112,128},... | collective-permute-start | bytes 221192 | tf_op jit(solution)/shard_map/while/body/eval_jaxpr/ppermute | solution.py:12
  340.9 3.5 collective-permute-start
  344.4 7.3 %collective-permute-start.1 = (f32[16,1152]{1,0:T(8,128)S(1)}, f32[16,1152]{1,0:T(8,128)S(1)}, u32[]{:S(2)}, u32[]{:S(2)}) collective-permute-start(f32[16,1152]{1,0:T(8,128)S(1)} %get-tuple-element.411), channel_id=1, source_target_pairs={{0,16},{16,32},{32,48},{48,64},{64,80},{80,96},{96,112},{112,128},... | collective-permute-start | bytes 221192 | tf_op jit(solution)/shard_map/while/body/eval_jaxpr/ppermute | solution.py:12
  352.9 3.5 collective-permute-start
  356.4 7.3 %collective-permute-start.1 = (f32[16,1152]{1,0:T(8,128)S(1)}, f32[16,1152]{1,0:T(8,128)S(1)}, u32[]{:S(2)}, u32[]{:S(2)}) collective-permute-start(f32[16,1152]{1,0:T(8,128)S(1)} %get-tuple-element.411), channel_id=1, source_target_pairs={{0,16},{16,32},{32,48},{48,64},{64,80},{80,96},{96,112},{112,128},... | collective-permute-start | bytes 221192 | tf_op jit(solution)/shard_map/while/body/eval_jaxpr/ppermute | solution.py:12
  365.0 3.5 collective-permute-start
  368.4 7.3 %collective-permute-start.1 = (f32[16,1152]{1,0:T(8,128)S(1)}, f32[16,1152]{1,0:T(8,128)S(1)}, u32[]{:S(2)}, u32[]{:S(2)}) collective-permute-start(f32[16,1152]{1,0:T(8,128)S(1)} %get-tuple-element.411), channel_id=1, source_target_pairs={{0,16},{16,32},{32,48},{48,64},{64,80},{80,96},{96,112},{112,128},... | collective-permute-start | bytes 221192 | tf_op jit(solution)/shard_map/while/body/eval_jaxpr/ppermute | solution.py:12
  377.0 3.5 collective-permute-start
  380.4 7.3 %collective-permute-start.1 = (f32[16,1152]{1,0:T(8,128)S(1)}, f32[16,1152]{1,0:T(8,128)S(1)}, u32[]{:S(2)}, u32[]{:S(2)}) collective-permute-start(f32[16,1152]{1,0:T(8,128)S(1)} %get-tuple-element.411), channel_id=1, source_target_pairs={{0,16},{16,32},{32,48},{48,64},{64,80},{80,96},{96,112},{112,128},... | collective-permute-start | bytes 221192 | tf_op jit(solution)/shard_map/while/body/eval_jaxpr/ppermute | solution.py:12
  397.2 89.8 %reduce-scatter.2.cloned.1.call-done = f32[16,1152]{1,0:T(8,128)} async-done(((f32[256,1152]{1,0:T(8,128)}), f32[16,1152]{1,0:T(8,128)}) %reduce-scatter.2.cloned.1.call-update) | async-done | bytes 73744 | tf_op jit(solution)/shard_map/reduce_scatter | solution.py:92
  (292 shorter events, 92.7 us)
Async XLA Ops:
  9.8 28.1 %all-to-all-start = ((bf16[16,16,1152]{2,1,0:T(8,128)(2,1)}), bf16[16,16,1152]{2,1,0:T(8,128)(2,1)S(1)}, u32[]{:S(2)}, u32[]{:S(2)}) async-start(bf16[16,16,1152]{2,1,0:T(8,128)(2,1)} %stack.2), calls=%async_computation | async-start | bytes 1179648 | tf_op jit(solution)/shard_map/all_to_all | solution.py:45
  21.2 465.8 %reduce-scatter.2.cloned.1.call-start = ((), (), s32[]{:S(2)}) async-start(), calls=%async_computation.2 | async-start | bytes 1253376 | tf_op jit(solution)/shard_map/reduce_scatter | solution.py:92
  46.3 9.6 %collective-permute-start = (bf16[16,1152]{1,0:T(8,128)(2,1)S(1)}, bf16[16,1152]{1,0:T(8,128)(2,1)S(1)}, u32[]{:S(2)}, u32[]{:S(2)}) collective-permute-start(bf16[16,1152]{1,0:T(8,128)(2,1)S(1)} %get-tuple-element.410), channel_id=1, source_target_pairs={{0,16},{16,32},{32,48},{48,64},{64,80},{80,96},{96,112},{112,128},... | collective-permute-start | bytes 110600 | tf_op jit(solution)/shard_map/while/body/eval_jaxpr/ppermute | solution.py:12
  48.4 8.5 %collective-permute-start.1 = (f32[16,1152]{1,0:T(8,128)S(1)}, f32[16,1152]{1,0:T(8,128)S(1)}, u32[]{:S(2)}, u32[]{:S(2)}) collective-permute-start(f32[16,1152]{1,0:T(8,128)S(1)} %get-tuple-element.411), channel_id=1, source_target_pairs={{0,16},{16,32},{32,48},{48,64},{64,80},{80,96},{96,112},{112,128},... | collective-permute-start | bytes 221192 | tf_op jit(solution)/shard_map/while/body/eval_jaxpr/ppermute | solution.py:12
  57.1 9.6 %collective-permute-start = (bf16[16,1152]{1,0:T(8,128)(2,1)S(1)}, bf16[16,1152]{1,0:T(8,128)(2,1)S(1)}, u32[]{:S(2)}, u32[]{:S(2)}) collective-permute-start(bf16[16,1152]{1,0:T(8,128)(2,1)S(1)} %get-tuple-element.410), channel_id=1, source_target_pairs={{0,16},{16,32},{32,48},{48,64},{64,80},{80,96},{96,112},{112,128},... | collective-permute-start | bytes 110600 | tf_op jit(solution)/shard_map/while/body/eval_jaxpr/ppermute | solution.py:12
  59.4 8.4 %collective-permute-start.1 = (f32[16,1152]{1,0:T(8,128)S(1)}, f32[16,1152]{1,0:T(8,128)S(1)}, u32[]{:S(2)}, u32[]{:S(2)}) collective-permute-start(f32[16,1152]{1,0:T(8,128)S(1)} %get-tuple-element.411), channel_id=1, source_target_pairs={{0,16},{16,32},{32,48},{48,64},{64,80},{80,96},{96,112},{112,128},... | collective-permute-start | bytes 221192 | tf_op jit(solution)/shard_map/while/body/eval_jaxpr/ppermute | solution.py:12
  67.9 9.6 %collective-permute-start = (bf16[16,1152]{1,0:T(8,128)(2,1)S(1)}, bf16[16,1152]{1,0:T(8,128)(2,1)S(1)}, u32[]{:S(2)}, u32[]{:S(2)}) collective-permute-start(bf16[16,1152]{1,0:T(8,128)(2,1)S(1)} %get-tuple-element.410), channel_id=1, source_target_pairs={{0,16},{16,32},{32,48},{48,64},{64,80},{80,96},{96,112},{112,128},... | collective-permute-start | bytes 110600 | tf_op jit(solution)/shard_map/while/body/eval_jaxpr/ppermute | solution.py:12
  70.2 8.4 %collective-permute-start.1 = (f32[16,1152]{1,0:T(8,128)S(1)}, f32[16,1152]{1,0:T(8,128)S(1)}, u32[]{:S(2)}, u32[]{:S(2)}) collective-permute-start(f32[16,1152]{1,0:T(8,128)S(1)} %get-tuple-element.411), channel_id=1, source_target_pairs={{0,16},{16,32},{32,48},{48,64},{64,80},{80,96},{96,112},{112,128},... | collective-permute-start | bytes 221192 | tf_op jit(solution)/shard_map/while/body/eval_jaxpr/ppermute | solution.py:12
  78.8 9.6 %collective-permute-start = (bf16[16,1152]{1,0:T(8,128)(2,1)S(1)}, bf16[16,1152]{1,0:T(8,128)(2,1)S(1)}, u32[]{:S(2)}, u32[]{:S(2)}) collective-permute-start(bf16[16,1152]{1,0:T(8,128)(2,1)S(1)} %get-tuple-element.410), channel_id=1, source_target_pairs={{0,16},{16,32},{32,48},{48,64},{64,80},{80,96},{96,112},{112,128},... | collective-permute-start | bytes 110600 | tf_op jit(solution)/shard_map/while/body/eval_jaxpr/ppermute | solution.py:12
  81.0 8.4 %collective-permute-start.1 = (f32[16,1152]{1,0:T(8,128)S(1)}, f32[16,1152]{1,0:T(8,128)S(1)}, u32[]{:S(2)}, u32[]{:S(2)}) collective-permute-start(f32[16,1152]{1,0:T(8,128)S(1)} %get-tuple-element.411), channel_id=1, source_target_pairs={{0,16},{16,32},{32,48},{48,64},{64,80},{80,96},{96,112},{112,128},... | collective-permute-start | bytes 221192 | tf_op jit(solution)/shard_map/while/body/eval_jaxpr/ppermute | solution.py:12
  89.6 9.6 %collective-permute-start = (bf16[16,1152]{1,0:T(8,128)(2,1)S(1)}, bf16[16,1152]{1,0:T(8,128)(2,1)S(1)}, u32[]{:S(2)}, u32[]{:S(2)}) collective-permute-start(bf16[16,1152]{1,0:T(8,128)(2,1)S(1)} %get-tuple-element.410), channel_id=1, source_target_pairs={{0,16},{16,32},{32,48},{48,64},{64,80},{80,96},{96,112},{112,128},... | collective-permute-start | bytes 110600 | tf_op jit(solution)/shard_map/while/body/eval_jaxpr/ppermute | solution.py:12
  91.8 8.4 %collective-permute-start.1 = (f32[16,1152]{1,0:T(8,128)S(1)}, f32[16,1152]{1,0:T(8,128)S(1)}, u32[]{:S(2)}, u32[]{:S(2)}) collective-permute-start(f32[16,1152]{1,0:T(8,128)S(1)} %get-tuple-element.411), channel_id=1, source_target_pairs={{0,16},{16,32},{32,48},{48,64},{64,80},{80,96},{96,112},{112,128},... | collective-permute-start | bytes 221192 | tf_op jit(solution)/shard_map/while/body/eval_jaxpr/ppermute | solution.py:12
  100.4 9.6 %collective-permute-start = (bf16[16,1152]{1,0:T(8,128)(2,1)S(1)}, bf16[16,1152]{1,0:T(8,128)(2,1)S(1)}, u32[]{:S(2)}, u32[]{:S(2)}) collective-permute-start(bf16[16,1152]{1,0:T(8,128)(2,1)S(1)} %get-tuple-element.410), channel_id=1, source_target_pairs={{0,16},{16,32},{32,48},{48,64},{64,80},{80,96},{96,112},{112,128},... | collective-permute-start | bytes 110600 | tf_op jit(solution)/shard_map/while/body/eval_jaxpr/ppermute | solution.py:12
  102.7 8.4 %collective-permute-start.1 = (f32[16,1152]{1,0:T(8,128)S(1)}, f32[16,1152]{1,0:T(8,128)S(1)}, u32[]{:S(2)}, u32[]{:S(2)}) collective-permute-start(f32[16,1152]{1,0:T(8,128)S(1)} %get-tuple-element.411), channel_id=1, source_target_pairs={{0,16},{16,32},{32,48},{48,64},{64,80},{80,96},{96,112},{112,128},... | collective-permute-start | bytes 221192 | tf_op jit(solution)/shard_map/while/body/eval_jaxpr/ppermute | solution.py:12
  111.2 9.6 %collective-permute-start = (bf16[16,1152]{1,0:T(8,128)(2,1)S(1)}, bf16[16,1152]{1,0:T(8,128)(2,1)S(1)}, u32[]{:S(2)}, u32[]{:S(2)}) collective-permute-start(bf16[16,1152]{1,0:T(8,128)(2,1)S(1)} %get-tuple-element.410), channel_id=1, source_target_pairs={{0,16},{16,32},{32,48},{48,64},{64,80},{80,96},{96,112},{112,128},... | collective-permute-start | bytes 110600 | tf_op jit(solution)/shard_map/while/body/eval_jaxpr/ppermute | solution.py:12
  113.5 8.4 %collective-permute-start.1 = (f32[16,1152]{1,0:T(8,128)S(1)}, f32[16,1152]{1,0:T(8,128)S(1)}, u32[]{:S(2)}, u32[]{:S(2)}) collective-permute-start(f32[16,1152]{1,0:T(8,128)S(1)} %get-tuple-element.411), channel_id=1, source_target_pairs={{0,16},{16,32},{32,48},{48,64},{64,80},{80,96},{96,112},{112,128},... | collective-permute-start | bytes 221192 | tf_op jit(solution)/shard_map/while/body/eval_jaxpr/ppermute | solution.py:12
  122.0 9.6 %collective-permute-start = (bf16[16,1152]{1,0:T(8,128)(2,1)S(1)}, bf16[16,1152]{1,0:T(8,128)(2,1)S(1)}, u32[]{:S(2)}, u32[]{:S(2)}) collective-permute-start(bf16[16,1152]{1,0:T(8,128)(2,1)S(1)} %get-tuple-element.410), channel_id=1, source_target_pairs={{0,16},{16,32},{32,48},{48,64},{64,80},{80,96},{96,112},{112,128},... | collective-permute-start | bytes 110600 | tf_op jit(solution)/shard_map/while/body/eval_jaxpr/ppermute | solution.py:12
  124.3 8.4 %collective-permute-start.1 = (f32[16,1152]{1,0:T(8,128)S(1)}, f32[16,1152]{1,0:T(8,128)S(1)}, u32[]{:S(2)}, u32[]{:S(2)}) collective-permute-start(f32[16,1152]{1,0:T(8,128)S(1)} %get-tuple-element.411), channel_id=1, source_target_pairs={{0,16},{16,32},{32,48},{48,64},{64,80},{80,96},{96,112},{112,128},... | collective-permute-start | bytes 221192 | tf_op jit(solution)/shard_map/while/body/eval_jaxpr/ppermute | solution.py:12
  132.9 10.5 %collective-permute-start = (bf16[16,1152]{1,0:T(8,128)(2,1)S(1)}, bf16[16,1152]{1,0:T(8,128)(2,1)S(1)}, u32[]{:S(2)}, u32[]{:S(2)}) collective-permute-start(bf16[16,1152]{1,0:T(8,128)(2,1)S(1)} %get-tuple-element.410), channel_id=1, source_target_pairs={{0,16},{16,32},{32,48},{48,64},{64,80},{80,96},{96,112},{112,128},... | collective-permute-start | bytes 110600 | tf_op jit(solution)/shard_map/while/body/eval_jaxpr/ppermute | solution.py:12
  135.8 8.6 %collective-permute-start.1 = (f32[16,1152]{1,0:T(8,128)S(1)}, f32[16,1152]{1,0:T(8,128)S(1)}, u32[]{:S(2)}, u32[]{:S(2)}) collective-permute-start(f32[16,1152]{1,0:T(8,128)S(1)} %get-tuple-element.411), channel_id=1, source_target_pairs={{0,16},{16,32},{32,48},{48,64},{64,80},{80,96},{96,112},{112,128},... | collective-permute-start | bytes 221192 | tf_op jit(solution)/shard_map/while/body/eval_jaxpr/ppermute | solution.py:12
  144.6 9.7 %collective-permute-start = (bf16[16,1152]{1,0:T(8,128)(2,1)S(1)}, bf16[16,1152]{1,0:T(8,128)(2,1)S(1)}, u32[]{:S(2)}, u32[]{:S(2)}) collective-permute-start(bf16[16,1152]{1,0:T(8,128)(2,1)S(1)} %get-tuple-element.410), channel_id=1, source_target_pairs={{0,16},{16,32},{32,48},{48,64},{64,80},{80,96},{96,112},{112,128},... | collective-permute-start | bytes 110600 | tf_op jit(solution)/shard_map/while/body/eval_jaxpr/ppermute | solution.py:12
  146.8 8.4 %collective-permute-start.1 = (f32[16,1152]{1,0:T(8,128)S(1)}, f32[16,1152]{1,0:T(8,128)S(1)}, u32[]{:S(2)}, u32[]{:S(2)}) collective-permute-start(f32[16,1152]{1,0:T(8,128)S(1)} %get-tuple-element.411), channel_id=1, source_target_pairs={{0,16},{16,32},{32,48},{48,64},{64,80},{80,96},{96,112},{112,128},... | collective-permute-start | bytes 221192 | tf_op jit(solution)/shard_map/while/body/eval_jaxpr/ppermute | solution.py:12
  155.4 10.0 %collective-permute-start = (bf16[16,1152]{1,0:T(8,128)(2,1)S(1)}, bf16[16,1152]{1,0:T(8,128)(2,1)S(1)}, u32[]{:S(2)}, u32[]{:S(2)}) collective-permute-start(bf16[16,1152]{1,0:T(8,128)(2,1)S(1)} %get-tuple-element.410), channel_id=1, source_target_pairs={{0,16},{16,32},{32,48},{48,64},{64,80},{80,96},{96,112},{112,128},... | collective-permute-start | bytes 110600 | tf_op jit(solution)/shard_map/while/body/eval_jaxpr/ppermute | solution.py:12
  158.0 8.5 %collective-permute-start.1 = (f32[16,1152]{1,0:T(8,128)S(1)}, f32[16,1152]{1,0:T(8,128)S(1)}, u32[]{:S(2)}, u32[]{:S(2)}) collective-permute-start(f32[16,1152]{1,0:T(8,128)S(1)} %get-tuple-element.411), channel_id=1, source_target_pairs={{0,16},{16,32},{32,48},{48,64},{64,80},{80,96},{96,112},{112,128},... | collective-permute-start | bytes 221192 | tf_op jit(solution)/shard_map/while/body/eval_jaxpr/ppermute | solution.py:12
  166.7 9.6 %collective-permute-start = (bf16[16,1152]{1,0:T(8,128)(2,1)S(1)}, bf16[16,1152]{1,0:T(8,128)(2,1)S(1)}, u32[]{:S(2)}, u32[]{:S(2)}) collective-permute-start(bf16[16,1152]{1,0:T(8,128)(2,1)S(1)} %get-tuple-element.410), channel_id=1, source_target_pairs={{0,16},{16,32},{32,48},{48,64},{64,80},{80,96},{96,112},{112,128},... | collective-permute-start | bytes 110600 | tf_op jit(solution)/shard_map/while/body/eval_jaxpr/ppermute | solution.py:12
  168.9 8.4 %collective-permute-start.1 = (f32[16,1152]{1,0:T(8,128)S(1)}, f32[16,1152]{1,0:T(8,128)S(1)}, u32[]{:S(2)}, u32[]{:S(2)}) collective-permute-start(f32[16,1152]{1,0:T(8,128)S(1)} %get-tuple-element.411), channel_id=1, source_target_pairs={{0,16},{16,32},{32,48},{48,64},{64,80},{80,96},{96,112},{112,128},... | collective-permute-start | bytes 221192 | tf_op jit(solution)/shard_map/while/body/eval_jaxpr/ppermute | solution.py:12
  177.5 9.6 %collective-permute-start = (bf16[16,1152]{1,0:T(8,128)(2,1)S(1)}, bf16[16,1152]{1,0:T(8,128)(2,1)S(1)}, u32[]{:S(2)}, u32[]{:S(2)}) collective-permute-start(bf16[16,1152]{1,0:T(8,128)(2,1)S(1)} %get-tuple-element.410), channel_id=1, source_target_pairs={{0,16},{16,32},{32,48},{48,64},{64,80},{80,96},{96,112},{112,128},... | collective-permute-start | bytes 110600 | tf_op jit(solution)/shard_map/while/body/eval_jaxpr/ppermute | solution.py:12
  188.3 9.6 %collective-permute-start = (bf16[16,1152]{1,0:T(8,128)(2,1)S(1)}, bf16[16,1152]{1,0:T(8,128)(2,1)S(1)}, u32[]{:S(2)}, u32[]{:S(2)}) collective-permute-start(bf16[16,1152]{1,0:T(8,128)(2,1)S(1)} %get-tuple-element.410), channel_id=1, source_target_pairs={{0,16},{16,32},{32,48},{48,64},{64,80},{80,96},{96,112},{112,128},... | collective-permute-start | bytes 110600 | tf_op jit(solution)/shard_map/while/body/eval_jaxpr/ppermute | solution.py:12
  199.2 9.6 %collective-permute-start = (bf16[16,1152]{1,0:T(8,128)(2,1)S(1)}, bf16[16,1152]{1,0:T(8,128)(2,1)S(1)}, u32[]{:S(2)}, u32[]{:S(2)}) collective-permute-start(bf16[16,1152]{1,0:T(8,128)(2,1)S(1)} %get-tuple-element.410), channel_id=1, source_target_pairs={{0,16},{16,32},{32,48},{48,64},{64,80},{80,96},{96,112},{112,128},... | collective-permute-start | bytes 110600 | tf_op jit(solution)/shard_map/while/body/eval_jaxpr/ppermute | solution.py:12
  210.0 9.6 %collective-permute-start = (bf16[16,1152]{1,0:T(8,128)(2,1)S(1)}, bf16[16,1152]{1,0:T(8,128)(2,1)S(1)}, u32[]{:S(2)}, u32[]{:S(2)}) collective-permute-start(bf16[16,1152]{1,0:T(8,128)(2,1)S(1)} %get-tuple-element.410), channel_id=1, source_target_pairs={{0,16},{16,32},{32,48},{48,64},{64,80},{80,96},{96,112},{112,128},... | collective-permute-start | bytes 110600 | tf_op jit(solution)/shard_map/while/body/eval_jaxpr/ppermute | solution.py:12
  220.8 10.6 %collective-permute-start = (bf16[16,1152]{1,0:T(8,128)(2,1)S(1)}, bf16[16,1152]{1,0:T(8,128)(2,1)S(1)}, u32[]{:S(2)}, u32[]{:S(2)}) collective-permute-start(bf16[16,1152]{1,0:T(8,128)(2,1)S(1)} %get-tuple-element.410), channel_id=1, source_target_pairs={{0,16},{16,32},{32,48},{48,64},{64,80},{80,96},{96,112},{112,128},... | collective-permute-start | bytes 110600 | tf_op jit(solution)/shard_map/while/body/eval_jaxpr/ppermute | solution.py:12
  224.1 8.4 %collective-permute-start.1 = (f32[16,1152]{1,0:T(8,128)S(1)}, f32[16,1152]{1,0:T(8,128)S(1)}, u32[]{:S(2)}, u32[]{:S(2)}) collective-permute-start(f32[16,1152]{1,0:T(8,128)S(1)} %get-tuple-element.411), channel_id=1, source_target_pairs={{0,16},{16,32},{32,48},{48,64},{64,80},{80,96},{96,112},{112,128},... | collective-permute-start | bytes 221192 | tf_op jit(solution)/shard_map/while/body/eval_jaxpr/ppermute | solution.py:12
  232.6 10.8 %collective-permute-start = (bf16[16,1152]{1,0:T(8,128)(2,1)S(1)}, bf16[16,1152]{1,0:T(8,128)(2,1)S(1)}, u32[]{:S(2)}, u32[]{:S(2)}) collective-permute-start(bf16[16,1152]{1,0:T(8,128)(2,1)S(1)} %get-tuple-element.410), channel_id=1, source_target_pairs={{0,16},{16,32},{32,48},{48,64},{64,80},{80,96},{96,112},{112,128},... | collective-permute-start | bytes 110600 | tf_op jit(solution)/shard_map/while/body/eval_jaxpr/ppermute | solution.py:12
  244.7 10.8 %collective-permute-start = (bf16[16,1152]{1,0:T(8,128)(2,1)S(1)}, bf16[16,1152]{1,0:T(8,128)(2,1)S(1)}, u32[]{:S(2)}, u32[]{:S(2)}) collective-permute-start(bf16[16,1152]{1,0:T(8,128)(2,1)S(1)} %get-tuple-element.410), channel_id=1, source_target_pairs={{0,16},{16,32},{32,48},{48,64},{64,80},{80,96},{96,112},{112,128},... | collective-permute-start | bytes 110600 | tf_op jit(solution)/shard_map/while/body/eval_jaxpr/ppermute | solution.py:12
  256.7 10.8 %collective-permute-start = (bf16[16,1152]{1,0:T(8,128)(2,1)S(1)}, bf16[16,1152]{1,0:T(8,128)(2,1)S(1)}, u32[]{:S(2)}, u32[]{:S(2)}) collective-permute-start(bf16[16,1152]{1,0:T(8,128)(2,1)S(1)} %get-tuple-element.410), channel_id=1, source_target_pairs={{0,16},{16,32},{32,48},{48,64},{64,80},{80,96},{96,112},{112,128},... | collective-permute-start | bytes 110600 | tf_op jit(solution)/shard_map/while/body/eval_jaxpr/ppermute | solution.py:12
  260.1 8.4 %collective-permute-start.1 = (f32[16,1152]{1,0:T(8,128)S(1)}, f32[16,1152]{1,0:T(8,128)S(1)}, u32[]{:S(2)}, u32[]{:S(2)}) collective-permute-start(f32[16,1152]{1,0:T(8,128)S(1)} %get-tuple-element.411), channel_id=1, source_target_pairs={{0,16},{16,32},{32,48},{48,64},{64,80},{80,96},{96,112},{112,128},... | collective-permute-start | bytes 221192 | tf_op jit(solution)/shard_map/while/body/eval_jaxpr/ppermute | solution.py:12
  268.7 10.8 %collective-permute-start = (bf16[16,1152]{1,0:T(8,128)(2,1)S(1)}, bf16[16,1152]{1,0:T(8,128)(2,1)S(1)}, u32[]{:S(2)}, u32[]{:S(2)}) collective-permute-start(bf16[16,1152]{1,0:T(8,128)(2,1)S(1)} %get-tuple-element.410), channel_id=1, source_target_pairs={{0,16},{16,32},{32,48},{48,64},{64,80},{80,96},{96,112},{112,128},... | collective-permute-start | bytes 110600 | tf_op jit(solution)/shard_map/while/body/eval_jaxpr/ppermute | solution.py:12
  280.7 10.8 %collective-permute-start = (bf16[16,1152]{1,0:T(8,128)(2,1)S(1)}, bf16[16,1152]{1,0:T(8,128)(2,1)S(1)}, u32[]{:S(2)}, u32[]{:S(2)}) collective-permute-start(bf16[16,1152]{1,0:T(8,128)(2,1)S(1)} %get-tuple-element.410), channel_id=1, source_target_pairs={{0,16},{16,32},{32,48},{48,64},{64,80},{80,96},{96,112},{112,128},... | collective-permute-start | bytes 110600 | tf_op jit(solution)/shard_map/while/body/eval_jaxpr/ppermute | solution.py:12
  292.8 10.8 %collective-permute-start = (bf16[16,1152]{1,0:T(8,128)(2,1)S(1)}, bf16[16,1152]{1,0:T(8,128)(2,1)S(1)}, u32[]{:S(2)}, u32[]{:S(2)}) collective-permute-start(bf16[16,1152]{1,0:T(8,128)(2,1)S(1)} %get-tuple-element.410), channel_id=1, source_target_pairs={{0,16},{16,32},{32,48},{48,64},{64,80},{80,96},{96,112},{112,128},... | collective-permute-start | bytes 110600 | tf_op jit(solution)/shard_map/while/body/eval_jaxpr/ppermute | solution.py:12
  296.2 8.4 %collective-permute-start.1 = (f32[16,1152]{1,0:T(8,128)S(1)}, f32[16,1152]{1,0:T(8,128)S(1)}, u32[]{:S(2)}, u32[]{:S(2)}) collective-permute-start(f32[16,1152]{1,0:T(8,128)S(1)} %get-tuple-element.411), channel_id=1, source_target_pairs={{0,16},{16,32},{32,48},{48,64},{64,80},{80,96},{96,112},{112,128},... | collective-permute-start | bytes 221192 | tf_op jit(solution)/shard_map/while/body/eval_jaxpr/ppermute | solution.py:12
  304.8 10.8 %collective-permute-start = (bf16[16,1152]{1,0:T(8,128)(2,1)S(1)}, bf16[16,1152]{1,0:T(8,128)(2,1)S(1)}, u32[]{:S(2)}, u32[]{:S(2)}) collective-permute-start(bf16[16,1152]{1,0:T(8,128)(2,1)S(1)} %get-tuple-element.410), channel_id=1, source_target_pairs={{0,16},{16,32},{32,48},{48,64},{64,80},{80,96},{96,112},{112,128},... | collective-permute-start | bytes 110600 | tf_op jit(solution)/shard_map/while/body/eval_jaxpr/ppermute | solution.py:12
  316.8 10.8 %collective-permute-start = (bf16[16,1152]{1,0:T(8,128)(2,1)S(1)}, bf16[16,1152]{1,0:T(8,128)(2,1)S(1)}, u32[]{:S(2)}, u32[]{:S(2)}) collective-permute-start(bf16[16,1152]{1,0:T(8,128)(2,1)S(1)} %get-tuple-element.410), channel_id=1, source_target_pairs={{0,16},{16,32},{32,48},{48,64},{64,80},{80,96},{96,112},{112,128},... | collective-permute-start | bytes 110600 | tf_op jit(solution)/shard_map/while/body/eval_jaxpr/ppermute | solution.py:12
  328.9 10.8 %collective-permute-start = (bf16[16,1152]{1,0:T(8,128)(2,1)S(1)}, bf16[16,1152]{1,0:T(8,128)(2,1)S(1)}, u32[]{:S(2)}, u32[]{:S(2)}) collective-permute-start(bf16[16,1152]{1,0:T(8,128)(2,1)S(1)} %get-tuple-element.410), channel_id=1, source_target_pairs={{0,16},{16,32},{32,48},{48,64},{64,80},{80,96},{96,112},{112,128},... | collective-permute-start | bytes 110600 | tf_op jit(solution)/shard_map/while/body/eval_jaxpr/ppermute | solution.py:12
  332.3 8.4 %collective-permute-start.1 = (f32[16,1152]{1,0:T(8,128)S(1)}, f32[16,1152]{1,0:T(8,128)S(1)}, u32[]{:S(2)}, u32[]{:S(2)}) collective-permute-start(f32[16,1152]{1,0:T(8,128)S(1)} %get-tuple-element.411), channel_id=1, source_target_pairs={{0,16},{16,32},{32,48},{48,64},{64,80},{80,96},{96,112},{112,128},... | collective-permute-start | bytes 221192 | tf_op jit(solution)/shard_map/while/body/eval_jaxpr/ppermute | solution.py:12
  340.9 10.8 %collective-permute-start = (bf16[16,1152]{1,0:T(8,128)(2,1)S(1)}, bf16[16,1152]{1,0:T(8,128)(2,1)S(1)}, u32[]{:S(2)}, u32[]{:S(2)}) collective-permute-start(bf16[16,1152]{1,0:T(8,128)(2,1)S(1)} %get-tuple-element.410), channel_id=1, source_target_pairs={{0,16},{16,32},{32,48},{48,64},{64,80},{80,96},{96,112},{112,128},... | collective-permute-start | bytes 110600 | tf_op jit(solution)/shard_map/while/body/eval_jaxpr/ppermute | solution.py:12
  352.9 10.8 %collective-permute-start = (bf16[16,1152]{1,0:T(8,128)(2,1)S(1)}, bf16[16,1152]{1,0:T(8,128)(2,1)S(1)}, u32[]{:S(2)}, u32[]{:S(2)}) collective-permute-start(bf16[16,1152]{1,0:T(8,128)(2,1)S(1)} %get-tuple-element.410), channel_id=1, source_target_pairs={{0,16},{16,32},{32,48},{48,64},{64,80},{80,96},{96,112},{112,128},... | collective-permute-start | bytes 110600 | tf_op jit(solution)/shard_map/while/body/eval_jaxpr/ppermute | solution.py:12
  365.0 10.8 %collective-permute-start = (bf16[16,1152]{1,0:T(8,128)(2,1)S(1)}, bf16[16,1152]{1,0:T(8,128)(2,1)S(1)}, u32[]{:S(2)}, u32[]{:S(2)}) collective-permute-start(bf16[16,1152]{1,0:T(8,128)(2,1)S(1)} %get-tuple-element.410), channel_id=1, source_target_pairs={{0,16},{16,32},{32,48},{48,64},{64,80},{80,96},{96,112},{112,128},... | collective-permute-start | bytes 110600 | tf_op jit(solution)/shard_map/while/body/eval_jaxpr/ppermute | solution.py:12
  377.0 10.8 %collective-permute-start = (bf16[16,1152]{1,0:T(8,128)(2,1)S(1)}, bf16[16,1152]{1,0:T(8,128)(2,1)S(1)}, u32[]{:S(2)}, u32[]{:S(2)}) collective-permute-start(bf16[16,1152]{1,0:T(8,128)(2,1)S(1)} %get-tuple-element.410), channel_id=1, source_target_pairs={{0,16},{16,32},{32,48},{48,64},{64,80},{80,96},{96,112},{112,128},... | collective-permute-start | bytes 110600 | tf_op jit(solution)/shard_map/while/body/eval_jaxpr/ppermute | solution.py:12
  (19 other events, 246.7 us)
Sparse Core Ops, SparseCore 0:
  390.7 96.2 reduce-scatter.1
